TPU v7x, 512 devices: a whole 4x8x8 slice. The times are simulated.
512 devices in a mesh: row: 16 (over z_lo, y), col: 32 (over x, z_hi, core).
Axes of the slice: x: 4, y: 8, z: 8 (z_hi: 4, z_lo: 2; z = z_hi * 2 + z_lo), core: 2. Of those that a mesh axis runs over, the one named last changes fastest.
Arguments:
- stored: float32 [16, 32, 8, 128, 128], P('row', 'col'), as said below
- pair_lists: int32 [16, 32, 3, 3, 128], P('row', 'col'), may hold values from 0 to 16, as said below
Outputs:
- square_tiles: float32 [16, 32, 8, 128, 128], P('row', 'col')
Inputs may be any that keep to these rules, and one draw needn't show every extreme that they name: stored[r, 2 j] holds the upper-triangle tiles of panel (r, j) and is zero where r > j; stored[r, 2 j + 1] equals stored[j, 2 r]. With j = c // 2 and k = (r + j + s) mod 16, an entry (x, y, t) of pair_lists[r, c, s] is real when t < 16: then x lies in the first 8 slots of panel_list(r, k) if r < k and in the last 8 if r > k, y likewise for panel_list(k, j). Other entries have all three indices equal to 16 and follow all real ones of their list. Some list has 128 real entries.
All inputs are finite; a program needn't handle non-finite values.
Results may differ from a plain program's by a relative error of at most 0.0003.
Values sent between devices are 32-bit elements; how exact they have to be, the bound alone decides.
No kernel may reach another device: no remote copies, remote signals or barrier semaphores. Data moves between devices by JAX's collectives and lax.ppermute only.
A program may use at most 64 MiB of HBM per device.

v0:
```python
import jax
import jax.numpy as jnp
from jax import lax
from jax.sharding import PartitionSpec as P

STEPS = 3


def shifted(block, axis, distance):
    devices = range(lax.axis_size(axis))
    route = [((i - distance) % len(devices), i) for i in devices]
    return lax.ppermute(block, axis, route)


def swapped(value, axis, apart):
    mask = 2**apart
    pairs = [(source, source ^ mask) for source in range(lax.axis_size(axis))]
    return lax.ppermute(value, axis, pairs)


def tile_block(left, right, entry, limit):
    first_idx = jnp.minimum(entry[0], limit - 1)
    second_idx = jnp.minimum(entry[1], limit - 1)
    a_tiles = jnp.take(left, first_idx, axis=0)
    b_tiles = jnp.take(right, second_idx, axis=0)
    blocks = jnp.einsum("pij,pjk->pik", a_tiles, b_tiles, precision=lax.Precision.HIGHEST)
    target = (entry[2][None, :] == jnp.arange(limit, dtype=jnp.int32)[:, None]).astype(jnp.float32)
    return jnp.einsum("tp,pik->tik", target, blocks, precision=lax.Precision.HIGHEST)


def along_col(values, amount):
    return shifted(values, "col", amount)


def along_row(values, amount):
    return shifted(values, "row", amount)


def across_cores(values):
    return swapped(values, "col", 0)


def on_device(stored, pair_lists):
    rows = lax.axis_size("row")
    cols = lax.axis_size("col")
    r_idx = lax.axis_index("row")
    c_idx = lax.axis_index("col")
    j_idx = c_idx // 2
    core = c_idx % 2
    mine = stored[0, 0]
    slots = mine.shape[0]
    limit = 2 * slots
    lists = pair_lists[0, 0]
    npair = lists.shape[2]
    digits = (rows - 1).bit_length()
    partner = across_cores(mine)
    upper = jnp.where(core == 0, mine, partner)
    mirror = jnp.where(core == 0, partner, mine)
    panel = jnp.concatenate([upper, jnp.swapaxes(mirror, 1, 2)], axis=0)
    values = panel
    for bit in range(digits):
        moved = along_col(values, cols - (2 << bit))
        values = jnp.where(r_idx >> bit & 1 == 1, moved, values)
    left = values
    values = panel
    for bit in range(digits):
        moved = along_row(values, rows - (1 << bit))
        values = jnp.where(j_idx >> bit & 1 == 1, moved, values)
    right = values
    total = jnp.zeros((limit, mine.shape[1], mine.shape[2]), jnp.float32)
    for step in range(STEPS):
        if step > 0:
            left = along_col(left, cols - 2)
            right = along_row(right, rows - 1)
        left_use = left
        right_use = right
        own_step = lists[step]

        def own_block(turn, acc, own_step=own_step, left_use=left_use, right_use=right_use):
            entry = lax.dynamic_slice_in_dim(own_step, turn * 16, 16, 1)
            return acc + tile_block(left_use, right_use, entry, limit)

        total = lax.fori_loop(0, npair // 16, own_block, total)
    kept = lax.dynamic_slice_in_dim(total, core * slots, slots, 0)
    sent = lax.dynamic_slice_in_dim(total, (1 - core) * slots, slots, 0)
    received = across_cores(sent)
    return (kept + received)[None, None]


def solution(mesh):
    return jax.shard_map(
        on_device,
        mesh=mesh,
        in_specs=(P("row", "col", None, None, None), P("row", "col", None, None, None)),
        out_specs=P("row", "col", None, None, None),
        check_vma=False,
    )
```

profile of v0, /device:TPU:1, one launch (start us, length us, event | category | flops | bytes accessed | tf_op | source)
XLA Modules:
  0.0 466.2 jit_solution(2735408010176613304)
XLA Ops:
  1.2 8.8 %collective-permute-start = (f32[8,128,128]{1,2,0:T(8,128)S(1)}, f32[8,128,128]{1,2,0:T(8,128)S(1)}, u32[]{:S(2)}, u32[]{:S(2)}) collective-permute-start(f32[8,128,128]{1,2,0:T(8,128)S(1)} %bitcast.61), channel_id=1, source_target_pairs={{0,1},{1,0},{2,3},{3,2},{4,5},{5,4},{6,7},{7,6},{8,9},{9,8},{10,11... | collective-permute-start | bytes 1572872 | tf_op jit(solution)/shard_map/ppermute | solution.py:18
  12.0 1.9 collective-permute-start.5
  13.9 11.6 %collective-permute-start.1 = (f32[16,128,128]{2,1,0:T(8,128)S(1)}, f32[16,128,128]{2,1,0:T(8,128)}, u32[]{:S(2)}, u32[]{:S(2)}) collective-permute-start(f32[16,128,128]{2,1,0:T(8,128)S(1)} %pad_maximum_fusion), channel_id=1, source_target_pairs={{2,0},{3,1},{4,2},{5,3},{6,4},{7,5},{8,6},{9,7},{10,8},{11,9},{12,... | collective-permute-start | bytes 3145736 | tf_op jit(solution)/shard_map/ppermute | solution.py:12
  25.5 12.8 %collective-permute-done.5 = f32[16,128,128]{2,1,0:T(8,128)S(1)} collective-permute-done((f32[16,128,128]{2,1,0:T(8,128)S(1)}, f32[16,128,128]{2,1,0:T(8,128)S(1)}, u32[]{:S(2)}, u32[]{:S(2)}) %collective-permute-start.5) | collective-permute-done | bytes 1048608 | tf_op jit(solution)/shard_map/ppermute | solution.py:12
  39.3 25.3 %collective-permute-done.1 = f32[16,128,128]{2,1,0:T(8,128)} collective-permute-done((f32[16,128,128]{2,1,0:T(8,128)S(1)}, f32[16,128,128]{2,1,0:T(8,128)}, u32[]{:S(2)}, u32[]{:S(2)}) %collective-permute-start.1) | collective-permute-done | bytes 1048608 | tf_op jit(solution)/shard_map/ppermute | solution.py:12
  64.8 9.3 %collective-permute-start.2 = (f32[16,128,128]{2,1,0:T(8,128)S(1)}, f32[16,128,128]{2,1,0:T(8,128)}, u32[]{:S(2)}, u32[]{:S(2)}) collective-permute-start(f32[16,128,128]{2,1,0:T(8,128)S(1)} %get-tuple-element.364), channel_id=1, source_target_pairs={{4,0},{5,1},{6,2},{7,3},{8,4},{9,5},{10,6},{11,7},{12,8},{13,9},{1... | collective-permute-start | bytes 3145736 | tf_op jit(solution)/shard_map/ppermute | solution.py:12
  74.1 1.9 collective-permute-start.6
  76.1 42.7 %collective-permute-done.2 = f32[16,128,128]{2,1,0:T(8,128)} collective-permute-done((f32[16,128,128]{2,1,0:T(8,128)S(1)}, f32[16,128,128]{2,1,0:T(8,128)}, u32[]{:S(2)}, u32[]{:S(2)}) %collective-permute-start.2) | collective-permute-done | bytes 1048608 | tf_op jit(solution)/shard_map/ppermute | solution.py:12
  118.9 1.9 collective-permute-start.3
  120.9 1.9 collective-permute-start.7
  122.9 21.3 %collective-permute-done.3 = f32[16,128,128]{2,1,0:T(8,128)} collective-permute-done((f32[16,128,128]{2,1,0:T(8,128)S(1)}, f32[16,128,128]{2,1,0:T(8,128)}, u32[]{:S(2)}, u32[]{:S(2)}) %collective-permute-start.3) | collective-permute-done | bytes 1048608 | tf_op jit(solution)/shard_map/ppermute | solution.py:12
  144.3 1.9 collective-permute-start.4
  147.6 21.0 %collective-permute-start.8 = (f32[16,128,128]{2,1,0:T(8,128)S(1)}, f32[16,128,128]{2,1,0:T(8,128)}, u32[]{:S(2)}, u32[]{:S(2)}) collective-permute-start(f32[16,128,128]{2,1,0:T(8,128)S(1)} %broadcast_select_fusion.2), channel_id=1, source_target_pairs={{256,0},{288,32},{320,64},{352,96},{384,128},{416,160},{448,192},{... | collective-permute-start | bytes 3145736 | tf_op jit(solution)/shard_map/ppermute | solution.py:12
  171.3 38.5 %collective-permute-start.9 = (f32[16,128,128]{2,1,0:T(8,128)}, f32[16,128,128]{2,1,0:T(8,128)}, u32[]{:S(2)}, u32[]{:S(2)}) collective-permute-start(f32[16,128,128]{2,1,0:T(8,128)} %broadcast_select_fusion.7), channel_id=1, source_target_pairs={{2,0},{3,1},{4,2},{5,3},{6,4},{7,5},{8,6},{9,7},{10,8},{11,9},{12,... | collective-permute-start | bytes 3145736 | tf_op jit(solution)/shard_map/ppermute | solution.py:12
  210.9 30.4 %collective-permute-start.10 = (f32[16,128,128]{2,1,0:T(8,128)}, f32[16,128,128]{2,1,0:T(8,128)}, u32[]{:S(2)}, u32[]{:S(2)}) collective-permute-start(f32[16,128,128]{2,1,0:T(8,128)} %broadcast_select_fusion.3), channel_id=1, source_target_pairs={{32,0},{64,32},{96,64},{128,96},{160,128},{192,160},{224,192},{256... | collective-permute-start | bytes 3145736 | tf_op jit(solution)/shard_map/ppermute | solution.py:12
  241.4 71.6 %while.42 = (s32[]{:T(128)}, f32[16,128,128]{2,0,1:T(8,128)S(1)}, s32[3,128]{1,0:T(4,128)S(1)}, f32[16,128,128]{2,1,0:T(8,128)}, f32[16,128,128]{2,1,0:T(8,128)}...) while((s32[]{:T(128)}, f32[16,128,128]{2,0,1:T(8,128)S(1)}, s32[3,128]{1,0:T(4,128)S(1)}, ...), condition=%wide.region_1.3_spmd.clone, body=%wide.region_0.2_spmd.clone.sunk | while | flops 454035936 | bytes 10495265 | solution.py:83
  241.5 1.8 gather_fusion.4
  243.3 2.9 gather_fusion.5
  246.2 2.5 fusion.63
  250.4 1.8 gather_fusion.4
  252.3 2.9 gather_fusion.5
  255.1 2.5 fusion.63
  259.4 1.8 gather_fusion.4
  261.2 2.9 gather_fusion.5
  264.1 2.5 fusion.63
  268.3 1.8 gather_fusion.4
  270.2 2.9 gather_fusion.5
  273.0 2.5 fusion.63
  277.3 1.8 gather_fusion.4
  279.1 2.9 gather_fusion.5
  282.0 2.5 fusion.63
  286.3 1.8 gather_fusion.4
  288.1 2.9 gather_fusion.5
  291.0 2.5 fusion.63
  295.2 1.8 gather_fusion.4
  297.1 2.9 gather_fusion.5
  299.9 2.5 fusion.63
  304.2 1.8 gather_fusion.4
  306.0 2.9 gather_fusion.5
  308.9 2.5 fusion.63
  313.0 9.2 %collective-permute-start.11 = (f32[16,128,128]{2,1,0:T(8,128)}, f32[16,128,128]{2,1,0:T(8,128)}, u32[]{:S(2)}, u32[]{:S(2)}) collective-permute-start(f32[16,128,128]{2,1,0:T(8,128)} %collective-permute-done.9), channel_id=1, source_target_pairs={{2,0},{3,1},{4,2},{5,3},{6,4},{7,5},{8,6},{9,7},{10,8},{11,9},{12,... | collective-permute-start | bytes 3145736 | tf_op jit(solution)/shard_map/ppermute | solution.py:12
  322.2 29.0 %collective-permute-start.12 = (f32[16,128,128]{2,1,0:T(8,128)}, f32[16,128,128]{2,1,0:T(8,128)}, u32[]{:S(2)}, u32[]{:S(2)}) collective-permute-start(f32[16,128,128]{2,1,0:T(8,128)} %collective-permute-done.10), channel_id=1, source_target_pairs={{32,0},{64,32},{96,64},{128,96},{160,128},{192,160},{224,192},{256... | collective-permute-start | bytes 3145736 | tf_op jit(solution)/shard_map/ppermute | solution.py:12
  351.2 52.7 %while.40 = (s32[]{:T(128)}, f32[16,128,128]{2,0,1:T(8,128)S(1)}, s32[3,128]{1,0:T(4,128)S(1)}, f32[16,128,128]{2,1,0:T(8,128)}, f32[16,128,128]{2,1,0:T(8,128)}...) while((s32[]{:T(128)}, f32[16,128,128]{2,0,1:T(8,128)S(1)}, s32[3,128]{1,0:T(4,128)S(1)}, ...), condition=%wide.region_3.5_spmd, body=%wide.region_2.4_spmd.sunk | while | flops 453773792 | bytes 10495255 | solution.py:83
  351.3 1.8 gather_fusion
  353.2 1.8 gather_fusion.1
  357.9 1.8 gather_fusion
  359.7 1.8 gather_fusion.1
  364.5 1.8 gather_fusion
  366.3 1.8 gather_fusion.1
  371.1 1.8 gather_fusion
  372.9 1.8 gather_fusion.1
  377.6 1.8 gather_fusion
  379.5 1.8 gather_fusion.1
  384.2 1.8 gather_fusion
  386.1 1.8 gather_fusion.1
  390.8 1.8 gather_fusion
  392.7 1.8 gather_fusion.1
  397.4 1.8 gather_fusion
  399.3 1.8 gather_fusion.1
  403.9 52.7 %while.41 = (s32[]{:T(128)}, f32[16,128,128]{2,0,1:T(8,128)S(1)}, s32[3,128]{1,0:T(4,128)S(1)}, f32[16,128,128]{2,1,0:T(8,128)}, f32[16,128,128]{2,1,0:T(8,128)}...) while((s32[]{:T(128)}, f32[16,128,128]{2,0,1:T(8,128)S(1)}, s32[3,128]{1,0:T(4,128)S(1)}, ...), condition=%wide.region_5.7_spmd, body=%wide.region_4.6_spmd.sunk | while | flops 453773792 | bytes 10495255 | solution.py:83
  404.0 1.8 gather_fusion.2
  405.9 1.8 gather_fusion.3
  410.6 1.8 gather_fusion.2
  457.0 6.8 %collective-permute-start.13 = (f32[8,128,128]{2,1,0:T(8,128)S(1)}, f32[8,128,128]{2,1,0:T(8,128)S(1)}, u32[]{:S(2)}, u32[]{:S(2)}) collective-permute-start(f32[8,128,128]{2,1,0:T(8,128)S(1)} %constant_dynamic-slice_fusion.3), channel_id=1, source_target_pairs={{0,1},{1,0},{2,3},{3,2},{4,5},{5,4},{6,7},{7,6},{8,9},{9,8},{10,11... | collective-permute-start | bytes 1572872 | tf_op jit(solution)/shard_map/ppermute | solution.py:18
  (184 shorter events, 95.6 us)
Async XLA Ops:
  1.2 10.3 %collective-permute-start = (f32[8,128,128]{1,2,0:T(8,128)S(1)}, f32[8,128,128]{1,2,0:T(8,128)S(1)}, u32[]{:S(2)}, u32[]{:S(2)}) collective-permute-start(f32[8,128,128]{1,2,0:T(8,128)S(1)} %bitcast.61), channel_id=1, source_target_pairs={{0,1},{1,0},{2,3},{3,2},{4,5},{5,4},{6,7},{7,6},{8,9},{9,8},{10,11... | collective-permute-start | bytes 1572872 | tf_op jit(solution)/shard_map/ppermute | solution.py:18
  12.0 26.4 %collective-permute-start.5 = (f32[16,128,128]{2,1,0:T(8,128)S(1)}, f32[16,128,128]{2,1,0:T(8,128)S(1)}, u32[]{:S(2)}, u32[]{:S(2)}) collective-permute-start(f32[16,128,128]{2,1,0:T(8,128)S(1)} %pad_maximum_fusion), channel_id=1, source_target_pairs={{32,0},{64,32},{96,64},{128,96},{160,128},{192,160},{224,192},{256... | collective-permute-start | bytes 3145736 | tf_op jit(solution)/shard_map/ppermute | solution.py:12
  13.9 50.8 %collective-permute-start.1 = (f32[16,128,128]{2,1,0:T(8,128)S(1)}, f32[16,128,128]{2,1,0:T(8,128)}, u32[]{:S(2)}, u32[]{:S(2)}) collective-permute-start(f32[16,128,128]{2,1,0:T(8,128)S(1)} %pad_maximum_fusion), channel_id=1, source_target_pairs={{2,0},{3,1},{4,2},{5,3},{6,4},{7,5},{8,6},{9,7},{10,8},{11,9},{12,... | collective-permute-start | bytes 3145736 | tf_op jit(solution)/shard_map/ppermute | solution.py:12
  38.3 1.0 copy-start.1
  64.8 53.9 %collective-permute-start.2 = (f32[16,128,128]{2,1,0:T(8,128)S(1)}, f32[16,128,128]{2,1,0:T(8,128)}, u32[]{:S(2)}, u32[]{:S(2)}) collective-permute-start(f32[16,128,128]{2,1,0:T(8,128)S(1)} %get-tuple-element.364), channel_id=1, source_target_pairs={{4,0},{5,1},{6,2},{7,3},{8,4},{9,5},{10,6},{11,7},{12,8},{13,9},{1... | collective-permute-start | bytes 3145736 | tf_op jit(solution)/shard_map/ppermute | solution.py:12
  74.1 46.6 %collective-permute-start.6 = (f32[16,128,128]{2,1,0:T(8,128)S(1)}, f32[16,128,128]{2,1,0:T(8,128)}, u32[]{:S(2)}, u32[]{:S(2)}) collective-permute-start(f32[16,128,128]{2,1,0:T(8,128)S(1)} %get-tuple-element.363), channel_id=1, source_target_pairs={{64,0},{96,32},{128,64},{160,96},{192,128},{224,160},{256,192},{28... | collective-permute-start | bytes 3145736 | tf_op jit(solution)/shard_map/ppermute | solution.py:12
  118.9 25.3 %collective-permute-start.3 = (f32[16,128,128]{2,1,0:T(8,128)S(1)}, f32[16,128,128]{2,1,0:T(8,128)}, u32[]{:S(2)}, u32[]{:S(2)}) collective-permute-start(f32[16,128,128]{2,1,0:T(8,128)S(1)} %broadcast_select_fusion.5), channel_id=1, source_target_pairs={{8,0},{9,1},{10,2},{11,3},{12,4},{13,5},{14,6},{15,7},{16,8},{17,9... | collective-permute-start | bytes 3145736 | tf_op jit(solution)/shard_map/ppermute | solution.py:12
  120.9 23.3 %copy-start = (f32[16,128,128]{2,1,0:T(8,128)}, f32[16,128,128]{2,1,0:T(8,128)S(1)}, u32[]{:S(2)}) copy-start(f32[16,128,128]{2,1,0:T(8,128)S(1)} %broadcast_select_fusion.1) | copy-start | bytes 3145732
  120.9 25.3 %collective-permute-start.7 = (f32[16,128,128]{2,1,0:T(8,128)S(1)}, f32[16,128,128]{2,1,0:T(8,128)}, u32[]{:S(2)}, u32[]{:S(2)}) collective-permute-start(f32[16,128,128]{2,1,0:T(8,128)S(1)} %broadcast_select_fusion.1), channel_id=1, source_target_pairs={{128,0},{160,32},{192,64},{224,96},{256,128},{288,160},{320,192},{... | collective-permute-start | bytes 3145736 | tf_op jit(solution)/shard_map/ppermute | solution.py:12
  144.3 25.9 %collective-permute-start.4 = (f32[16,128,128]{2,1,0:T(8,128)S(1)}, f32[16,128,128]{2,1,0:T(8,128)}, u32[]{:S(2)}, u32[]{:S(2)}) collective-permute-start(f32[16,128,128]{2,1,0:T(8,128)S(1)} %broadcast_select_fusion.6), channel_id=1, source_target_pairs={{16,0},{17,1},{18,2},{19,3},{20,4},{21,5},{22,6},{23,7},{24,8},{25... | collective-permute-start | bytes 3145736 | tf_op jit(solution)/shard_map/ppermute | solution.py:12
  147.6 62.2 %collective-permute-start.8 = (f32[16,128,128]{2,1,0:T(8,128)S(1)}, f32[16,128,128]{2,1,0:T(8,128)}, u32[]{:S(2)}, u32[]{:S(2)}) collective-permute-start(f32[16,128,128]{2,1,0:T(8,128)S(1)} %broadcast_select_fusion.2), channel_id=1, source_target_pairs={{256,0},{288,32},{320,64},{352,96},{384,128},{416,160},{448,192},{... | collective-permute-start | bytes 3145736 | tf_op jit(solution)/shard_map/ppermute | solution.py:12
  168.6 0.7 copy-start.2
  171.3 141.7 %collective-permute-start.9 = (f32[16,128,128]{2,1,0:T(8,128)}, f32[16,128,128]{2,1,0:T(8,128)}, u32[]{:S(2)}, u32[]{:S(2)}) collective-permute-start(f32[16,128,128]{2,1,0:T(8,128)} %broadcast_select_fusion.7), channel_id=1, source_target_pairs={{2,0},{3,1},{4,2},{5,3},{6,4},{7,5},{8,6},{9,7},{10,8},{11,9},{12,... | collective-permute-start | bytes 3145736 | tf_op jit(solution)/shard_map/ppermute | solution.py:12
  210.9 111.3 %collective-permute-start.10 = (f32[16,128,128]{2,1,0:T(8,128)}, f32[16,128,128]{2,1,0:T(8,128)}, u32[]{:S(2)}, u32[]{:S(2)}) collective-permute-start(f32[16,128,128]{2,1,0:T(8,128)} %broadcast_select_fusion.3), channel_id=1, source_target_pairs={{32,0},{64,32},{96,64},{128,96},{160,128},{192,160},{224,192},{256... | collective-permute-start | bytes 3145736 | tf_op jit(solution)/shard_map/ppermute | solution.py:12
  313.0 90.9 %collective-permute-start.11 = (f32[16,128,128]{2,1,0:T(8,128)}, f32[16,128,128]{2,1,0:T(8,128)}, u32[]{:S(2)}, u32[]{:S(2)}) collective-permute-start(f32[16,128,128]{2,1,0:T(8,128)} %collective-permute-done.9), channel_id=1, source_target_pairs={{2,0},{3,1},{4,2},{5,3},{6,4},{7,5},{8,6},{9,7},{10,8},{11,9},{12,... | collective-permute-start | bytes 3145736 | tf_op jit(solution)/shard_map/ppermute | solution.py:12
  322.2 81.7 %collective-permute-start.12 = (f32[16,128,128]{2,1,0:T(8,128)}, f32[16,128,128]{2,1,0:T(8,128)}, u32[]{:S(2)}, u32[]{:S(2)}) collective-permute-start(f32[16,128,128]{2,1,0:T(8,128)} %collective-permute-done.10), channel_id=1, source_target_pairs={{32,0},{64,32},{96,64},{128,96},{160,128},{192,160},{224,192},{256... | collective-permute-start | bytes 3145736 | tf_op jit(solution)/shard_map/ppermute | solution.py:12
  457.0 8.3 %collective-permute-start.13 = (f32[8,128,128]{2,1,0:T(8,128)S(1)}, f32[8,128,128]{2,1,0:T(8,128)S(1)}, u32[]{:S(2)}, u32[]{:S(2)}) collective-permute-start(f32[8,128,128]{2,1,0:T(8,128)S(1)} %constant_dynamic-slice_fusion.3), channel_id=1, source_target_pairs={{0,1},{1,0},{2,3},{3,2},{4,5},{5,4},{6,7},{7,6},{8,9},{9,8},{10,11... | collective-permute-start | bytes 1572872 | tf_op jit(solution)/shard_map/ppermute | solution.py:18
where the time goes:
time: 469 us; the launch traced here: 466 us
  starting transfers between devices  174 us (37%)
  waiting for transfers between devices  106 us (23%)
  local copies, waits for them, and re-layouts  102 us (22%)
  matrix products  76.7 us (16%)
  other arithmetic  5.6 us (1%)
    ppermute x12, starting transfers between devices, shifted(): return lax.ppermute(block, axis, route)  159 us
    ppermute x12, waiting for transfers between devices, shifted(): return lax.ppermute(block, axis, route)  103 us
    gather x24, local copies, waits for them, and re-layouts, tile_block(): a_tiles = jnp.take(left, first_idx, axis=0)  52.2 us
    gather x24, local copies, waits for them, and re-layouts, tile_block(): b_tiles = jnp.take(right, second_idx, axis=0)  44.1 us
    dot_general x24, matrix products, tile_block(): jnp.einsum('pij,pjk->pik', a_tiles, b_tiles, precision=lax.Precision.HIGH...  40.3 us
    dot_general x24, matrix products, tile_block(): jnp.einsum('tp,pik->tik', target, blocks, precision=lax.Precision.HIGHEST)  36.4 us
    ppermute x2, starting transfers between devices, swapped(): return lax.ppermute(value, axis, pairs)  15.6 us
  transfers between devices with their start and end apart: 14, of which 7 were waited for; matrix products, arithmetic and copies ran while one was open for 27% of the time, Pallas kernels for 0%

commit v1 on v0

v1 whole, which is shorter than its diff:
```python
import jax
import jax.numpy as jnp
from jax import lax
from jax.experimental import pallas as pl
from jax.experimental.pallas import tpu as pltpu
from jax.sharding import PartitionSpec as P

STEPS = 3
GRID = 16
SU = 8
BS = 128
NPAIR = 128
AXES = ("row", "col")


def device(r, j, core):
    return (r * GRID + j) * 2 + core


def data_core(a, b):
    return 0 if a <= b else 1


def left_plan(r, j, phase):
    low = r < 8
    if phase == 0:
        step = 0 if low else 2
    elif phase == 1:
        step = 2 if low else 0
    else:
        step = 1
    if phase < 2:
        return step, (r, (r + j + step) % GRID)
    return step, (r, (j + 1) % GRID if low else (j - 1) % GRID)


def right_order(j):
    m = j % 8
    if m <= 2:
        return (0, 1, 2)
    if m in (3, 7):
        return (1, 0, 2)
    return (2, 1, 0)


def right_plan(r, j, phase):
    m = j % 8
    if phase == 0:
        step = right_order(j)[0]
        return step, ((r + j + step) % GRID, j)
    if m in (3, 7):
        step = (2 if r % 2 == 0 else 0) if phase == 1 else (0 if r % 2 == 0 else 2)
        return step, ((r + 1) % GRID if step == 2 else (r - 1) % GRID, j)
    return right_order(j)[phase], ((r + 1) % GRID if m <= 2 else (r - 1) % GRID, j)


def route(phase):
    pairs = []
    for r in range(GRID):
        for j in range(GRID):
            pairs.append((device(*left_plan(r, j, phase)[1], 0), device(r, j, 0)))
            pairs.append((device(*right_plan(r, j, phase)[1], 1), device(r, j, 1)))
    return pairs


def init_route():
    out = []
    for a in range(GRID):
        for b in range(GRID):
            core = data_core(a, b)
            out.append((device(a, b, core), device(a, b, 1 - core)))
    return out


def swap_route():
    return [(d, d ^ 1) for d in range(2 * GRID * GRID)]


def bucket_kernel(core_ref, own_ref, other_ref, codes_ref, counts_ref):
    core = core_ref[0]
    for step in range(STEPS):
        for t in range(SU + 1):
            counts_ref[step, t] = 0
        for ref in (own_ref, other_ref):

            def more(i, ref=ref, step=step):
                return jnp.logical_and(i < NPAIR, ref[step, 2, jnp.minimum(i, NPAIR - 1)] < 2 * SU)

            def put(i, ref=ref, step=step):
                x = jnp.minimum(ref[step, 0, i], 2 * SU - 1)
                y = jnp.minimum(ref[step, 1, i], 2 * SU - 1)
                t = ref[step, 2, i] - core * SU
                mine = jnp.logical_and(t >= 0, t < SU)
                slot = jnp.where(mine, t, SU)
                n = counts_ref[step, slot]
                codes_ref[step, slot, n] = y * (2 * SU) + x
                counts_ref[step, slot] = n + 1
                return i + 1

            lax.while_loop(more, put, jnp.int32(0))


def bucket(core, own, other):
    smem = pl.BlockSpec(memory_space=pltpu.SMEM)
    return pl.pallas_call(
        bucket_kernel,
        out_shape=(
            jax.ShapeDtypeStruct((STEPS, SU + 1, 2 * NPAIR), jnp.int32),
            jax.ShapeDtypeStruct((STEPS, 16), jnp.int32),
        ),
        in_specs=[smem, smem, smem],
        out_specs=(smem, smem),
        cost_estimate=pl.CostEstimate(flops=4_000_000, bytes_accessed=60_000, transcendentals=0),
    )(core, own, other)


def product_kernel(step, first, *refs):
    if first:
        where_ref, codes_ref, counts_ref, left_ref, right_ref, out_ref, lhs, rhs, prod = refs
    else:
        where_ref, codes_ref, counts_ref, left_ref, right_ref, acc_ref, out_ref, lhs, rhs, prod = refs
    r = where_ref[0]
    j = where_ref[1]
    k = lax.rem(r + j + step, GRID)

    def load_left(flip):
        for x in range(SU):
            tile = left_ref[x]
            if flip:
                tile = tile.T
            high = tile.astype(jnp.bfloat16)
            low = (tile - high.astype(jnp.float32)).astype(jnp.bfloat16)
            rows = slice(x * BS, (x + 1) * BS)
            lhs[rows, 0:BS] = high
            lhs[rows, BS : 2 * BS] = high
            lhs[rows, 2 * BS : 3 * BS] = low

    def load_right(flip):
        for y in range(SU):
            tile = right_ref[y]
            if flip:
                tile = tile.T
            high = tile.astype(jnp.bfloat16)
            low = (tile - high.astype(jnp.float32)).astype(jnp.bfloat16)
            cols = slice(y * BS, (y + 1) * BS)
            rhs[0:BS, cols] = high
            rhs[BS : 2 * BS, cols] = low
            rhs[2 * BS : 3 * BS, cols] = high

    def multiply(v, w):
        for yp in range(SU // 2):
            b = rhs[:, yp * 2 * BS : (yp + 1) * 2 * BS]
            for xp in range(SU // 2):
                a = lhs[xp * 2 * BS : (xp + 1) * 2 * BS, :]
                res = jnp.dot(a, b, preferred_element_type=jnp.float32)
                rows = slice((v * SU + 2 * xp) * BS, (v * SU + 2 * xp + 2) * BS)
                prod[w * SU + 2 * yp, rows, :] = res[:, :BS]
                prod[w * SU + 2 * yp + 1, rows, :] = res[:, BS:]

    def left_needed(v):
        return r <= k if v == 0 else r >= k

    def right_needed(w):
        return k <= j if w == 0 else k >= j

    for v in (0, 1):

        @pl.when(left_needed(v))
        def _(v=v):
            load_left(v == 1)
            for w in (0, 1):

                @pl.when(right_needed(w))
                def _(v=v, w=w):
                    load_right(w == 1)
                    multiply(v, w)

    for t in range(SU):
        if first:
            acc = jnp.zeros((BS, BS), jnp.float32)
        else:
            acc = acc_ref[t]

        def add(i, acc, t=t):
            code = codes_ref[step, t, i]
            y = code // (2 * SU)
            x = lax.rem(code, 2 * SU)
            return acc + prod[y, pl.ds(pl.multiple_of(x * BS, BS), BS), :]

        out_ref[t] = lax.fori_loop(0, counts_ref[step, t], add, acc)


def product(step, where, codes, counts, left, right, acc):
    smem = pl.BlockSpec(memory_space=pltpu.SMEM)
    vmem = pl.BlockSpec(memory_space=pltpu.VMEM)
    first = acc is None

    def kernel(*refs):
        product_kernel(step, first, *refs)

    args = (where, codes, counts, left, right) + (() if first else (acc,))
    return pl.pallas_call(
        kernel,
        out_shape=jax.ShapeDtypeStruct((SU, BS, BS), jnp.float32),
        in_specs=[smem, smem, smem, vmem, vmem] + ([] if first else [vmem]),
        out_specs=vmem,
        scratch_shapes=[
            pltpu.VMEM((SU * BS, 3 * BS), jnp.bfloat16),
            pltpu.VMEM((3 * BS, SU * BS), jnp.bfloat16),
            pltpu.VMEM((2 * SU, 2 * SU * BS, BS), jnp.float32),
        ],
        compiler_params=pltpu.CompilerParams(vmem_limit_bytes=32 * 1024 * 1024),
        cost_estimate=pl.CostEstimate(flops=3_000_000_000, bytes_accessed=1_500_000, transcendentals=0),
    )(*args)


def on_device(stored, pair_lists):
    r = lax.axis_index("row")
    c = lax.axis_index("col")
    j = c // 2
    core = c % 2
    mine = stored[0, 0]
    lists = pair_lists[0, 0]

    partner = lax.ppermute(mine, AXES, init_route())
    home = jnp.where((core == 0) == (r <= j), mine, partner)
    got0 = lax.ppermute(home, AXES, route(0))
    other_lists = lax.ppermute(lists, AXES, swap_route())
    codes, counts = bucket(core.astype(jnp.int32)[None], lists, other_lists)
    right_side = core == 1
    send1 = jnp.where(right_side, got0, home)
    got1 = lax.ppermute(send1, AXES, route(1))
    low = r < 8
    middle = (j % 8 == 3) | (j % 8 == 7)
    send2 = jnp.where(right_side, jnp.where(middle, got0, got1), got0)
    got2 = lax.ppermute(send2, AXES, route(2))
    swaps = [lax.ppermute(g, AXES, swap_route()) for g in (got0, got1, got2)]
    gots = [got0, got1, got2]

    lefts = [jnp.where(right_side, s, g) for s, g in zip(swaps, gots)]
    rights = [jnp.where(right_side, g, s) for s, g in zip(swaps, gots)]
    left = [
        jnp.where(low, lefts[0], lefts[1]),
        lefts[2],
        jnp.where(low, lefts[1], lefts[0]),
    ]
    up = j % 8 <= 2
    even = r % 2 == 0
    right = [
        jnp.where(middle, jnp.where(even, rights[2], rights[1]), jnp.where(up, rights[0], rights[2])),
        jnp.where(middle, rights[0], rights[1]),
        jnp.where(middle, jnp.where(even, rights[1], rights[2]), jnp.where(up, rights[2], rights[0])),
    ]
    where = jnp.stack([r, j]).astype(jnp.int32)
    acc = None
    for step in range(STEPS):
        acc = product(step, where, codes, counts, left[step], right[step], acc)
    return acc[None, None]


def solution(mesh):
    return jax.shard_map(
        on_device,
        mesh=mesh,
        in_specs=(P("row", "col", None, None, None), P("row", "col", None, None, None)),
        out_specs=P("row", "col", None, None, None),
        check_vma=False,
    )
```

time: 469 us -> 95.2 us (0.20)
  the two profiles are of different devices: /device:TPU:1 before, /device:TPU:321 now
where the time goes in v1:
time: 95.2 us; the launch traced here: 94.8 us
  starting transfers between devices  43.7 us (46%)
  Pallas kernels  25.7 us (27%)
  waiting for transfers between devices  22 us (23%)
  other arithmetic  1.91 us (2%)
  local copies, waits for them, and re-layouts  1.29 us (1%)
    ppermute x3, starting transfers between devices, on_device(): swaps = [lax.ppermute(g, AXES, swap_route()) for g in (got0, got1, got2)]  20.7 us
    pallas_call x3, Pallas kernels, product(): pl.pallas_call(kernel, out_shape=jax.ShapeDtypeStruct((SU, BS, BS), jnp.f...  13.3 us
    pallas_call x1, Pallas kernels, bucket(): pl.pallas_call(bucket_kernel, out_shape=(jax.ShapeDtypeStruct((STEPS, SU...  12.4 us
    ppermute x1, waiting for transfers between devices, on_device(): got0 = lax.ppermute(home, AXES, route(0))  11.7 us
    ppermute x1, waiting for transfers between devices, on_device(): got1 = lax.ppermute(send1, AXES, route(1))  7.51 us
    ppermute x1, starting transfers between devices, on_device(): got2 = lax.ppermute(send2, AXES, route(2))  7.47 us
    ppermute x1, starting transfers between devices, on_device(): got0 = lax.ppermute(home, AXES, route(0))  5.87 us
    ppermute x1, starting transfers between devices, on_device(): got1 = lax.ppermute(send1, AXES, route(1))  5.11 us
  transfers between devices with their start and end apart: 8, of which 4 were waited for; matrix products, arithmetic and copies ran while one was open for 0% of the time, Pallas kernels for 13%

profile of v1, /device:TPU:321, one launch (start us, length us, event | category | flops | bytes accessed | tf_op | source)
XLA Modules:
  0.0 94.8 jit_solution(12782376388345895714)
XLA Ops:
  0.0 2.6 %collective-permute-start.1 = (f32[8,128,128]{2,1,0:T(8,128)}, f32[8,128,128]{2,1,0:T(8,128)S(1)}, u32[]{:S(2)}, u32[]{:S(2)}) collective-permute-start(f32[8,128,128]{2,1,0:T(8,128)} %bitcast.9), channel_id=1, source_target_pairs={{0,1},{2,3},{4,5},{6,7},{8,9},{10,11},{12,13},{14,15},{16,17},{18,... | collective-permute-start | bytes 1572872 | tf_op jit(solution)/shard_map/ppermute | solution.py:225
  2.6 1.7 %collective-permute-done.1 = f32[8,128,128]{2,1,0:T(8,128)S(1)} collective-permute-done((f32[8,128,128]{2,1,0:T(8,128)}, f32[8,128,128]{2,1,0:T(8,128)S(1)}, u32[]{:S(2)}, u32[]{:S(2)}) %collective-permute-start.1) | collective-permute-done | bytes 524320 | tf_op jit(solution)/shard_map/ppermute | solution.py:225
  4.3 1.1 %broadcast_select_fusion.1 = f32[8,128,128]{2,1,0:T(8,128)S(1)} fusion(f32[8,128,128]{2,1,0:T(8,128)S(1)} %collective-permute-done.1, pred[]{:T(512)S(6)} %eq.26, f32[1,1,8,128,128]{4,3,2,1,0:T(8,128)} %param.2), kind=kLoop, calls=%fused_computation.4 | loop fusion | flops 131072 | bytes 1572865 | tf_op jit(solution)/shard_map/jit(_where)/select_n | solution.py:226
  5.4 5.9 %collective-permute-start.2 = (f32[8,128,128]{2,1,0:T(8,128)S(1)}, f32[8,128,128]{2,1,0:T(8,128)S(1)}, u32[]{:S(2)}, u32[]{:S(2)}) collective-permute-start(f32[8,128,128]{2,1,0:T(8,128)S(1)} %broadcast_select_fusion.1), channel_id=1, source_target_pairs={{0,0},{1,1},{2,2},{35,3},{4,4},{69,5},{6,6},{135,7},{8,8},{201,9},... | collective-permute-start | bytes 1572872 | tf_op jit(solution)/shard_map/ppermute | solution.py:227
  11.3 11.7 %collective-permute-done.2 = f32[8,128,128]{2,1,0:T(8,128)S(1)} collective-permute-done((f32[8,128,128]{2,1,0:T(8,128)S(1)}, f32[8,128,128]{2,1,0:T(8,128)S(1)}, u32[]{:S(2)}, u32[]{:S(2)}) %collective-permute-start.2) | collective-permute-done | bytes 524320 | tf_op jit(solution)/shard_map/ppermute | solution.py:227
  23.0 0.1 broadcast_select_fusion.8
  23.1 5.1 %collective-permute-start.3 = (f32[8,128,128]{2,1,0:T(8,128)S(1)}, f32[8,128,128]{2,1,0:T(8,128)S(1)}, u32[]{:S(2)}, u32[]{:S(2)}) collective-permute-start(f32[8,128,128]{2,1,0:T(8,128)S(1)} %broadcast_select_fusion.8), channel_id=1, source_target_pairs={{4,0},{33,1},{6,2},{35,3},{8,4},{37,5},{10,6},{39,7},{12,8},{489,9... | collective-permute-start | bytes 1572872 | tf_op jit(solution)/shard_map/ppermute | solution.py:232
  28.2 0.0 copy-start.3
  28.2 7.5 %collective-permute-done.3 = f32[8,128,128]{2,1,0:T(8,128)S(1)} collective-permute-done((f32[8,128,128]{2,1,0:T(8,128)S(1)}, f32[8,128,128]{2,1,0:T(8,128)S(1)}, u32[]{:S(2)}, u32[]{:S(2)}) %collective-permute-start.3) | collective-permute-done | bytes 524320 | tf_op jit(solution)/shard_map/ppermute | solution.py:232
  35.7 0.1 select_select_fusion
  35.8 7.5 %collective-permute-start.6 = (f32[8,128,128]{2,1,0:T(8,128)S(1)}, f32[8,128,128]{2,1,0:T(8,128)S(1)}, u32[]{:S(2)}, u32[]{:S(2)}) collective-permute-start(f32[8,128,128]{2,1,0:T(8,128)S(1)} %select_select_fusion), channel_id=1, source_target_pairs={{2,0},{33,1},{4,2},{35,3},{6,4},{37,5},{8,6},{487,7},{10,8},{489,9... | collective-permute-start | bytes 1572872 | tf_op jit(solution)/shard_map/ppermute | solution.py:236
  43.3 11.8 %collective-permute-start.5 = (f32[8,128,128]{2,1,0:T(8,128)S(1)}, f32[8,128,128]{2,1,0:T(8,128)S(1)}, u32[]{:S(2)}, u32[]{:S(2)}) collective-permute-start(f32[8,128,128]{2,1,0:T(8,128)S(1)} %collective-permute-done.2), channel_id=1, source_target_pairs={{0,1},{1,0},{2,3},{3,2},{4,5},{5,4},{6,7},{7,6},{8,9},{9,8},{10,11... | collective-permute-start | bytes 1572872 | tf_op jit(solution)/shard_map/ppermute | solution.py:237
  55.1 1.9 %collective-permute-start.4 = (f32[8,128,128]{2,1,0:T(8,128)S(1)}, f32[8,128,128]{2,1,0:T(8,128)S(1)}, u32[]{:S(2)}, u32[]{:S(2)}) collective-permute-start(f32[8,128,128]{2,1,0:T(8,128)S(1)} %collective-permute-done.3), channel_id=1, source_target_pairs={{0,1},{1,0},{2,3},{3,2},{4,5},{5,4},{6,7},{7,6},{8,9},{9,8},{10,11... | collective-permute-start | bytes 1572872 | tf_op jit(solution)/shard_map/ppermute | solution.py:237
  57.0 0.0 collective-permute-done.6
  57.0 7.0 %collective-permute-start.7 = (f32[8,128,128]{2,1,0:T(8,128)S(1)}, f32[8,128,128]{2,1,0:T(8,128)S(1)}, u32[]{:S(2)}, u32[]{:S(2)}) collective-permute-start(f32[8,128,128]{2,1,0:T(8,128)S(1)} %collective-permute-done.6), channel_id=1, source_target_pairs={{0,1},{1,0},{2,3},{3,2},{4,5},{5,4},{6,7},{7,6},{8,9},{9,8},{10,11... | collective-permute-start | bytes 1572872 | tf_op jit(solution)/shard_map/ppermute | solution.py:237
  64.0 0.0 copy-done.3
  64.1 0.0 copy-start.2
  64.1 1.9 %collective-permute-start = (s32[3,3,128]{2,1,0:T(4,128)S(1)}, s32[3,3,128]{2,1,0:T(4,128)S(1)}, u32[]{:S(2)}, u32[]{:S(2)}) collective-permute-start(s32[3,3,128]{2,1,0:T(4,128)S(1)} %bitcast.10), channel_id=1, source_target_pairs={{0,1},{1,0},{2,3},{3,2},{4,5},{5,4},{6,7},{7,6},{8,9},{9,8},{10,11... | collective-permute-start | bytes 13832 | tf_op jit(solution)/shard_map/ppermute | solution.py:228
  66.0 0.1 pad_add_fusion.refs_0_
  66.1 0.0 copy-done.2
  66.1 1.1 %collective-permute-done.other_ref = s32[3,3,128]{2,1,0:T(4,128)S(1)} collective-permute-done((s32[3,3,128]{2,1,0:T(4,128)S(1)}, s32[3,3,128]{2,1,0:T(4,128)S(1)}, u32[]{:S(2)}, u32[]{:S(2)}) %collective-permute-start) | collective-permute-done | bytes 4640 | tf_op jit(solution)/shard_map/ppermute | solution.py:228
  67.1 0.0 copy-start.4
  67.1 0.6 copy-done.4
  67.7 12.4 %shard_map.28 = (s32[3,9,256]{2,1,0:T(8,128)}, s32[3,16]{1,0:T(4,128)}) custom-call(s32[1]{0:T(128)} %bitcast.2.core_ref, s32[3,3,128]{2,1,0:T(4,128)} %bitcast.11, s32[3,3,128]{2,1,0:T(4,128)} %copy-done.4), custom_call_target="tpu_custom_call" | custom-call | flops 4000000 | bytes 60000 | tf_op jit(solution)/shard_map/pallas_call | solution.py:105
  80.2 0.0 copy-start
  80.2 0.0 collective-permute-done.5
  80.2 0.0 collective-permute-done.4
  80.2 0.0 collective-permute-done.7
  80.2 0.5 select_select_fusion.1
  80.7 0.0 copy-start.1
  80.7 0.3 copy-done
  81.0 0.4 copy-done.1
  81.4 4.9 %shard_map.29.refs_5_ = f32[8,128,128]{2,1,0:T(8,128)S(1)} custom-call(s32[2]{0:T(128)S(1)} %pad_add_fusion.refs_0_, s32[3,9,256]{2,1,0:T(8,128)S(1)} %copy-done, s32[3,16]{1,0:T(4,128)S(1)} %copy-done.1, f32[8,128,128]{2,1,0:T(8,128)S(1)} %get-tuple-element.12.refs_3_, f32[8,128,128]{2,1,0:T(8,128)S(1)} %get-tuple-element.9.refs_4_), custom_call_target="tpu_custom_call" | custom-call | flops 3000000000 | bytes 1500000 | tf_op jit(solution)/shard_map/pallas_call | solution.py:202
  86.2 0.2 broadcast_select_fusion
  86.4 3.3 %shard_map.30.refs_5_ = f32[8,128,128]{2,1,0:T(8,128)S(1)} custom-call(s32[2]{0:T(128)S(1)} %pad_add_fusion.refs_0_, s32[3,9,256]{2,1,0:T(8,128)S(1)} %copy-done, s32[3,16]{1,0:T(4,128)S(1)} %copy-done.1, f32[8,128,128]{2,1,0:T(8,128)S(1)} %get-tuple-element.14.refs_3_, f32[8,128,128]{2,1,0:T(8,128)S(1)} %get-tuple-element.15.refs_4_, ...), custom_call_target="tpu_custom_call" | custom-call | flops 3000000000 | bytes 1500000 | tf_op jit(solution)/shard_map/pallas_call | solution.py:202
  89.8 5.1 %shard_map.31 = f32[8,128,128]{2,1,0:T(8,128)} custom-call(s32[2]{0:T(128)S(1)} %pad_add_fusion.refs_0_, s32[3,9,256]{2,1,0:T(8,128)S(1)} %copy-done, s32[3,16]{1,0:T(4,128)S(1)} %copy-done.1, f32[8,128,128]{2,1,0:T(8,128)S(1)} %get-tuple-element.13.refs_3_, f32[8,128,128]{2,1,0:T(8,128)S(1)} %get-tuple-element.16.refs_4_, f32[8,128,128]{2,1,0:T(8,128)S(1)} %shard_map.30.refs_5_), custom_call_target="tpu_custom_call" | custom-call | flops 3000000000 | bytes 1500000 | tf_op jit(solution)/shard_map/pallas_call | solution.py:202
  (1 shorter events, 0.0 us)
Async XLA Ops:
  0.0 4.3 %collective-permute-start.1 = (f32[8,128,128]{2,1,0:T(8,128)}, f32[8,128,128]{2,1,0:T(8,128)S(1)}, u32[]{:S(2)}, u32[]{:S(2)}) collective-permute-start(f32[8,128,128]{2,1,0:T(8,128)} %bitcast.9), channel_id=1, source_target_pairs={{0,1},{2,3},{4,5},{6,7},{8,9},{10,11},{12,13},{14,15},{16,17},{18,... | collective-permute-start | bytes 1572872 | tf_op jit(solution)/shard_map/ppermute | solution.py:225
  5.4 17.6 %collective-permute-start.2 = (f32[8,128,128]{2,1,0:T(8,128)S(1)}, f32[8,128,128]{2,1,0:T(8,128)S(1)}, u32[]{:S(2)}, u32[]{:S(2)}) collective-permute-start(f32[8,128,128]{2,1,0:T(8,128)S(1)} %broadcast_select_fusion.1), channel_id=1, source_target_pairs={{0,0},{1,1},{2,2},{35,3},{4,4},{69,5},{6,6},{135,7},{8,8},{201,9},... | collective-permute-start | bytes 1572872 | tf_op jit(solution)/shard_map/ppermute | solution.py:227
  23.1 12.7 %collective-permute-start.3 = (f32[8,128,128]{2,1,0:T(8,128)S(1)}, f32[8,128,128]{2,1,0:T(8,128)S(1)}, u32[]{:S(2)}, u32[]{:S(2)}) collective-permute-start(f32[8,128,128]{2,1,0:T(8,128)S(1)} %broadcast_select_fusion.8), channel_id=1, source_target_pairs={{4,0},{33,1},{6,2},{35,3},{8,4},{37,5},{10,6},{39,7},{12,8},{489,9... | collective-permute-start | bytes 1572872 | tf_op jit(solution)/shard_map/ppermute | solution.py:232
  28.2 35.8 %copy-start.3 = (s32[1,1,3,3,128]{4,1,3,2,0:T(1,128)S(1)}, s32[1,1,3,3,128]{4,1,3,2,0:T(1,128)}, u32[]{:S(2)}) copy-start(s32[1,1,3,3,128]{4,1,3,2,0:T(1,128)} %param.3) | copy-start | bytes 13828
  35.8 21.2 %collective-permute-start.6 = (f32[8,128,128]{2,1,0:T(8,128)S(1)}, f32[8,128,128]{2,1,0:T(8,128)S(1)}, u32[]{:S(2)}, u32[]{:S(2)}) collective-permute-start(f32[8,128,128]{2,1,0:T(8,128)S(1)} %select_select_fusion), channel_id=1, source_target_pairs={{2,0},{33,1},{4,2},{35,3},{6,4},{37,5},{8,6},{487,7},{10,8},{489,9... | collective-permute-start | bytes 1572872 | tf_op jit(solution)/shard_map/ppermute | solution.py:236
  43.3 36.9 %collective-permute-start.5 = (f32[8,128,128]{2,1,0:T(8,128)S(1)}, f32[8,128,128]{2,1,0:T(8,128)S(1)}, u32[]{:S(2)}, u32[]{:S(2)}) collective-permute-start(f32[8,128,128]{2,1,0:T(8,128)S(1)} %collective-permute-done.2), channel_id=1, source_target_pairs={{0,1},{1,0},{2,3},{3,2},{4,5},{5,4},{6,7},{7,6},{8,9},{9,8},{10,11... | collective-permute-start | bytes 1572872 | tf_op jit(solution)/shard_map/ppermute | solution.py:237
  55.1 25.1 %collective-permute-start.4 = (f32[8,128,128]{2,1,0:T(8,128)S(1)}, f32[8,128,128]{2,1,0:T(8,128)S(1)}, u32[]{:S(2)}, u32[]{:S(2)}) collective-permute-start(f32[8,128,128]{2,1,0:T(8,128)S(1)} %collective-permute-done.3), channel_id=1, source_target_pairs={{0,1},{1,0},{2,3},{3,2},{4,5},{5,4},{6,7},{7,6},{8,9},{9,8},{10,11... | collective-permute-start | bytes 1572872 | tf_op jit(solution)/shard_map/ppermute | solution.py:237
  57.0 23.2 %collective-permute-start.7 = (f32[8,128,128]{2,1,0:T(8,128)S(1)}, f32[8,128,128]{2,1,0:T(8,128)S(1)}, u32[]{:S(2)}, u32[]{:S(2)}) collective-permute-start(f32[8,128,128]{2,1,0:T(8,128)S(1)} %collective-permute-done.6), channel_id=1, source_target_pairs={{0,1},{1,0},{2,3},{3,2},{4,5},{5,4},{6,7},{7,6},{8,9},{9,8},{10,11... | collective-permute-start | bytes 1572872 | tf_op jit(solution)/shard_map/ppermute | solution.py:237
  64.1 2.0 %copy-start.2 = (s32[1,1,3,3,128]{4,3,1,2,0:T(4,128)}, s32[1,1,3,3,128]{4,3,1,2,0:T(4,128)S(1)}, u32[]{:S(2)}) copy-start(s32[1,1,3,3,128]{4,3,1,2,0:T(4,128)S(1)} %copy.5) | copy-start | bytes 13828
  64.1 3.1 %collective-permute-start = (s32[3,3,128]{2,1,0:T(4,128)S(1)}, s32[3,3,128]{2,1,0:T(4,128)S(1)}, u32[]{:S(2)}, u32[]{:S(2)}) collective-permute-start(s32[3,3,128]{2,1,0:T(4,128)S(1)} %bitcast.10), channel_id=1, source_target_pairs={{0,1},{1,0},{2,3},{3,2},{4,5},{5,4},{6,7},{7,6},{8,9},{9,8},{10,11... | collective-permute-start | bytes 13832 | tf_op jit(solution)/shard_map/ppermute | solution.py:228
  67.1 0.6 copy-start.4
  80.2 0.8 copy-start
  80.7 0.7 copy-start.1

commit v2 on v0

v2 whole, which is shorter than its diff:
```python
import jax
import jax.numpy as jnp
from jax import lax
from jax.experimental import pallas as pl
from jax.experimental.pallas import tpu as pltpu
from jax.sharding import PartitionSpec as P

STEPS = 3
GRID = 16
SU = 8
BS = 128
NPAIR = 128
AXES = ("row", "col")
CHUNK = 4
UNROLL = 2


def device(r, j, core):
    return (r * GRID + j) * 2 + core


def data_core(a, b):
    return 0 if a <= b else 1


def left_route(step, to_core):
    return [
        (device(r, (r + j + step) % GRID, data_core(r, (r + j + step) % GRID)), device(r, j, to_core))
        for r in range(GRID)
        for j in range(GRID)
    ]


def right_route(step, to_core):
    return [
        (device((r + j + step) % GRID, j, data_core((r + j + step) % GRID, j)), device(r, j, to_core))
        for r in range(GRID)
        for j in range(GRID)
    ]


def near_route(shift, to_core):
    return [(device((r + shift) % GRID, j, 1), device(r, j, to_core)) for r in range(GRID) for j in range(GRID)]


def swap_route():
    return [(d, d ^ 1) for d in range(2 * GRID * GRID)]


def bucket_kernel(core_ref, own_ref, other_ref, codes_ref, counts_ref):
    core = core_ref[0]
    groups = ((1, 2 * SU), (2 * core, 2 * SU))
    for group, (_, slots) in enumerate(groups):
        for t in range(slots + 1):
            counts_ref[group, t] = 0
    for ref in (own_ref, other_ref):

        def more(i, ref=ref):
            at = jnp.minimum(i, NPAIR - CHUNK)
            real = jnp.logical_or(ref[groups[0][0], 2, at] < 2 * SU, ref[groups[1][0], 2, at] < 2 * SU)
            return jnp.logical_and(i < NPAIR, real)

        def put(i, ref=ref):
            for n in range(CHUNK):
                for group, (step, slots) in enumerate(groups):
                    x = jnp.minimum(ref[step, 0, i + n], 2 * SU - 1)
                    y = jnp.minimum(ref[step, 1, i + n], 2 * SU - 1)
                    t = ref[step, 2, i + n]
                    slot = jnp.where(t < 2 * SU, jnp.bitwise_xor(t, core * SU), 2 * SU)
                    slot = jnp.minimum(slot, slots)
                    m = counts_ref[group, slot]
                    codes_ref[group, slot, m] = y * (2 * SU) + x
                    counts_ref[group, slot] = m + 1
            return i + CHUNK

        lax.while_loop(more, put, jnp.int32(0))
    for group, (_, slots) in enumerate(groups):
        for t in range(slots):
            m = counts_ref[group, t]
            for n in range(UNROLL - 1):
                codes_ref[group, t, m + n] = 4 * SU * SU
            counts_ref[group, t] = (m + UNROLL - 1) // UNROLL


def bucket(core, own, other):
    smem = pl.BlockSpec(memory_space=pltpu.SMEM)
    return pl.pallas_call(
        bucket_kernel,
        out_shape=(
            jax.ShapeDtypeStruct((2, 2 * SU + 1, 2 * NPAIR + 128), jnp.int32),
            jax.ShapeDtypeStruct((2, 2 * SU + 1), jnp.int32),
        ),
        in_specs=[smem, smem, smem],
        out_specs=(smem, smem),
        cost_estimate=pl.CostEstimate(flops=1000, bytes_accessed=1000, transcendentals=0),
    )(core, own, other)


def product_kernel(group, where_ref, codes_ref, counts_ref, left_ref, right_ref, *refs):
    if group == 0:
        out_ref, lhs, rhs, prod = refs
    else:
        acc_ref, own_ref, sent_ref, lhs, rhs, prod = refs
    r = where_ref[0]
    j = where_ref[1]
    core = where_ref[2]
    k = lax.rem(r + j + (1 if group == 0 else 2 * core), GRID)

    def halves(tile):
        high = tile.astype(jnp.bfloat16)
        return high, (tile - high.astype(jnp.float32)).astype(jnp.bfloat16)

    def load_left(flip):
        for x in range(SU):
            high, low = halves(left_ref[x].T if flip else left_ref[x])
            rows = slice(x * BS, (x + 1) * BS)
            lhs[rows, 0:BS] = high
            lhs[rows, BS : 2 * BS] = high
            lhs[rows, 2 * BS : 3 * BS] = low

    def load_right(flip):
        for y in range(SU):
            high, low = halves(right_ref[y].T if flip else right_ref[y])
            cols = slice(y * BS, (y + 1) * BS)
            rhs[0:BS, cols] = high
            rhs[BS : 2 * BS, cols] = low
            rhs[2 * BS : 3 * BS, cols] = high

    def multiply(v, w):
        for yp in range(SU // 2):
            b = rhs[:, yp * 2 * BS : (yp + 1) * 2 * BS]
            for xp in range(SU // 2):
                a = lhs[xp * 2 * BS : (xp + 1) * 2 * BS, :]
                res = jnp.dot(a, b, preferred_element_type=jnp.float32)
                rows = slice((v * SU + 2 * xp) * BS, (v * SU + 2 * xp + 2) * BS)
                prod[w * SU + 2 * yp, rows, :] = res[:, :BS]
                prod[w * SU + 2 * yp + 1, rows, :] = res[:, BS:]

    def make_products():
        prod[2 * SU, 0:BS, :] = jnp.zeros((BS, BS), jnp.float32)
        for v in (0, 1):

            @pl.when(r <= k if v == 0 else r >= k)
            def _(v=v):
                load_left(v == 1)
                for w in (0, 1):

                    @pl.when(k <= j if w == 0 else k >= j)
                    def _(v=v, w=w):
                        load_right(w == 1)
                        multiply(v, w)

    def total(t, acc):
        def add(i, acc):
            for n in range(UNROLL):
                code = codes_ref[group, t, UNROLL * i + n]
                y = lax.shift_right_logical(code, 4)
                x = jnp.bitwise_and(code, 15)
                acc = acc + prod[y, pl.ds(pl.multiple_of(x * BS, BS), BS), :]
            return acc

        return lax.fori_loop(0, counts_ref[group, t], add, acc)

    if group == 0:

        @pl.when(core == 0)
        def _():
            out_ref[...] = jnp.zeros_like(out_ref)

        @pl.when(core == 1)
        def _():
            make_products()
            for t in range(2 * SU):
                out_ref[t] = total(t, jnp.zeros((BS, BS), jnp.float32))

    else:
        make_products()
        for t in range(SU):
            own_ref[t] = total(t, acc_ref[t])
        for t in range(SU):
            sent_ref[t] = total(SU + t, acc_ref[SU + t])


def product(group, where, codes, counts, left, right, acc):
    smem = pl.BlockSpec(memory_space=pltpu.SMEM)
    vmem = pl.BlockSpec(memory_space=pltpu.VMEM)
    tiles = jax.ShapeDtypeStruct((SU, BS, BS), jnp.float32)

    def kernel(*refs):
        product_kernel(group, *refs)

    args = (where, codes, counts, left, right) + (() if group == 0 else (acc,))
    return pl.pallas_call(
        kernel,
        out_shape=jax.ShapeDtypeStruct((2 * SU, BS, BS), jnp.float32) if group == 0 else (tiles, tiles),
        in_specs=[smem, smem, smem, vmem, vmem] + [vmem] * group,
        out_specs=vmem if group == 0 else (vmem, vmem),
        scratch_shapes=[
            pltpu.VMEM((SU * BS, 3 * BS), jnp.bfloat16),
            pltpu.VMEM((3 * BS, SU * BS), jnp.bfloat16),
            pltpu.VMEM((2 * SU + 1, 2 * SU * BS, BS), jnp.float32),
        ],
        compiler_params=pltpu.CompilerParams(vmem_limit_bytes=32 * 1024 * 1024),
        cost_estimate=pl.CostEstimate(flops=1000, bytes_accessed=1000, transcendentals=0),
    )(*args)


def on_device(stored, pair_lists):
    r = lax.axis_index("row")
    c = lax.axis_index("col")
    j = c // 2
    core = c % 2
    mine = stored[0, 0]
    lists = pair_lists[0, 0]
    low = core == 0

    middle = lax.ppermute(mine, AXES, right_route(1, 1))
    left1 = lax.ppermute(mine, AXES, left_route(1, 1))
    left0 = lax.ppermute(mine, AXES, left_route(0, 0))
    left2 = lax.ppermute(mine, AXES, left_route(2, 1))
    right0 = lax.ppermute(middle, AXES, near_route(-1, 0))
    right2 = lax.ppermute(middle, AXES, near_route(1, 1))

    other_lists = lax.ppermute(lists, AXES, swap_route())
    codes, counts = bucket(core.astype(jnp.int32)[None], lists, other_lists)
    where = jnp.stack([r, j, core]).astype(jnp.int32)
    acc = product(0, where, codes, counts, left1, middle, None)
    kept, sent = product(
        1, where, codes, counts, jnp.where(low, left0, left2), jnp.where(low, right0, right2), acc
    )
    return (kept + lax.ppermute(sent, AXES, swap_route()))[None, None]


def solution(mesh):
    return jax.shard_map(
        on_device,
        mesh=mesh,
        in_specs=(P("row", "col", None, None, None), P("row", "col", None, None, None)),
        out_specs=P("row", "col", None, None, None),
        check_vma=False,
    )
```

time: 469 us -> 59.7 us (0.13)
  the two profiles are of different devices: /device:TPU:1 before, /device:TPU:193 now
where the time goes in v2:
time: 59.7 us; the launch traced here: 59.2 us
  starting transfers between devices  34 us (57%)
  Pallas kernels  13.1 us (22%)
  waiting for transfers between devices  8.63 us (14%)
  local copies, waits for them, and re-layouts  2.24 us (4%)
  other arithmetic  1.06 us (2%)
    ppermute x1, starting transfers between devices, on_device(): right0 = lax.ppermute(middle, AXES, near_route(-1, 0))  9.07 us
    pallas_call x2, Pallas kernels, product(): pl.pallas_call(kernel, out_shape=jax.ShapeDtypeStruct((2 * SU, BS, BS), j...  7.75 us
    ppermute x1, starting transfers between devices, on_device(): left2 = lax.ppermute(mine, AXES, left_route(2, 1))  6.97 us
    ppermute x1, waiting for transfers between devices, on_device(): left2 = lax.ppermute(mine, AXES, left_route(2, 1))  6.74 us
    pallas_call x1, Pallas kernels, bucket(): pl.pallas_call(bucket_kernel, out_shape=(jax.ShapeDtypeStruct((2, 2 * SU...  5.39 us
    ppermute x1, starting transfers between devices, on_device(): left0 = lax.ppermute(mine, AXES, left_route(0, 0))  5.3 us
    ppermute x1, starting transfers between devices, on_device(): middle = lax.ppermute(mine, AXES, right_route(1, 1))  4.96 us
    unnamed x9, local copies, waits for them, and re-layouts  2.24 us
  transfers between devices with their start and end apart: 8, of which 2 were waited for; matrix products, arithmetic and copies ran while one was open for 1% of the time, Pallas kernels for 15%

profile of v2, /device:TPU:193, one launch (start us, length us, event | category | flops | bytes accessed | tf_op | source)
XLA Modules:
  0.0 59.2 jit_solution(872882613879262843)
XLA Ops:
  0.0 5.0 %collective-permute-start.3 = (f32[8,128,128]{2,1,0:T(8,128)}, f32[8,128,128]{2,1,0:T(8,128)S(1)}, u32[]{:S(2)}, u32[]{:S(2)}) collective-permute-start(f32[8,128,128]{2,1,0:T(8,128)} %bitcast.11), channel_id=1, source_target_pairs={{33,1},{67,3},{101,5},{135,7},{169,9},{203,11},{237,13},{271,15},{... | collective-permute-start | bytes 1572872 | tf_op jit(solution)/shard_map/ppermute | solution.py:217
  5.0 1.9 %collective-permute-start.6 = (f32[8,128,128]{2,1,0:T(8,128)}, f32[8,128,128]{2,1,0:T(8,128)S(1)}, u32[]{:S(2)}, u32[]{:S(2)}) collective-permute-start(f32[8,128,128]{2,1,0:T(8,128)} %bitcast.12), channel_id=1, source_target_pairs={{2,1},{4,3},{6,5},{8,7},{10,9},{12,11},{14,13},{16,15},{18,17},{20... | collective-permute-start | bytes 1572872 | tf_op jit(solution)/shard_map/ppermute | solution.py:218
  6.9 5.3 %collective-permute-start.1 = (f32[8,128,128]{2,1,0:T(8,128)}, f32[8,128,128]{2,1,0:T(8,128)S(1)}, u32[]{:S(2)}, u32[]{:S(2)}) collective-permute-start(f32[8,128,128]{2,1,0:T(8,128)} %bitcast.13), channel_id=1, source_target_pairs={{0,0},{2,2},{4,4},{6,6},{8,8},{10,10},{12,12},{14,14},{16,16},{18,... | collective-permute-start | bytes 1572872 | tf_op jit(solution)/shard_map/ppermute | solution.py:219
  12.2 7.0 %collective-permute-start.2 = (f32[8,128,128]{2,1,0:T(8,128)}, f32[8,128,128]{2,1,0:T(8,128)S(1)}, u32[]{:S(2)}, u32[]{:S(2)}) collective-permute-start(f32[8,128,128]{2,1,0:T(8,128)} %bitcast.14), channel_id=1, source_target_pairs={{4,1},{6,3},{8,5},{10,7},{12,9},{14,11},{16,13},{18,15},{20,17},{2... | collective-permute-start | bytes 1572872 | tf_op jit(solution)/shard_map/ppermute | solution.py:220
  19.2 0.7 %copy.5 = s32[1,1,3,3,128]{4,3,1,2,0:T(4,128)S(1)} copy(s32[1,1,3,3,128]{4,1,3,2,0:T(1,128)} %param.3) | data formatting | bytes 9216
  19.9 0.0 copy-start.2
  19.9 1.9 %collective-permute-start = (s32[3,3,128]{2,1,0:T(4,128)S(1)}, s32[3,3,128]{2,1,0:T(4,128)S(1)}, u32[]{:S(2)}, u32[]{:S(2)}) collective-permute-start(s32[3,3,128]{2,1,0:T(4,128)S(1)} %bitcast.9), channel_id=1, source_target_pairs={{0,1},{1,0},{2,3},{3,2},{4,5},{5,4},{6,7},{7,6},{8,9},{9,8},{10,11... | collective-permute-start | bytes 13832 | tf_op jit(solution)/shard_map/ppermute | solution.py:224
  21.8 0.0 collective-permute-done.3.refs_4_
  21.8 9.1 %collective-permute-start.4 = (f32[8,128,128]{2,1,0:T(8,128)S(1)}, f32[8,128,128]{2,1,0:T(8,128)S(1)}, u32[]{:S(2)}, u32[]{:S(2)}) collective-permute-start(f32[8,128,128]{2,1,0:T(8,128)S(1)} %collective-permute-done.3.refs_4_), channel_id=1, source_target_pairs={{481,0},{483,2},{485,4},{487,6},{489,8},{491,10},{493,12},{495,14}... | collective-permute-start | bytes 1572872 | tf_op jit(solution)/shard_map/ppermute | solution.py:221
  30.9 0.0 collective-permute-done.other_ref
  30.9 0.0 copy-start.3
  30.9 1.9 %collective-permute-start.5 = (f32[8,128,128]{2,1,0:T(8,128)S(1)}, f32[8,128,128]{2,1,0:T(8,128)S(1)}, u32[]{:S(2)}, u32[]{:S(2)}) collective-permute-start(f32[8,128,128]{2,1,0:T(8,128)S(1)} %collective-permute-done.3.refs_4_), channel_id=1, source_target_pairs={{33,1},{35,3},{37,5},{39,7},{41,9},{43,11},{45,13},{47,15},{49,17}... | collective-permute-start | bytes 1572872 | tf_op jit(solution)/shard_map/ppermute | solution.py:222
  32.8 0.0 copy-done.2
  32.8 0.0 copy-done.3
  32.9 0.1 pad_add_fusion.refs_0_
  32.9 5.4 %shard_map.28 = (s32[2,17,384]{2,1,0:T(8,128)}, s32[2,17]{1,0:T(2,128)}) custom-call(s32[1]{0:T(128)} %bitcast.2.core_ref, s32[3,3,128]{2,1,0:T(4,128)} %bitcast.10, s32[3,3,128]{2,1,0:T(4,128)} %copy-done.3), custom_call_target="tpu_custom_call" | custom-call | flops 1000 | bytes 1000 | tf_op jit(solution)/shard_map/pallas_call | solution.py:87
  38.3 0.0 collective-permute-done.6.refs_3_
  38.4 0.0 copy-start.1
  38.4 0.7 %copy-done.1 = s32[2,17]{1,0:T(2,128)S(1)} copy-done((s32[2,17]{1,0:T(2,128)S(1)}, s32[2,17]{1,0:T(2,128)}, u32[]{:S(2)}) %copy-start.1) | copy-done | bytes 160
  39.0 0.0 copy-start
  39.0 0.9 %copy-done = s32[2,17,384]{2,1,0:T(8,128)S(1)} copy-done((s32[2,17,384]{2,1,0:T(8,128)S(1)}, s32[2,17,384]{2,1,0:T(8,128)}, u32[]{:S(2)}) %copy-start) | copy-done | bytes 52248
  39.9 3.8 %shard_map.29.refs_5_ = f32[16,128,128]{2,1,0:T(8,128)S(1)} custom-call(s32[3]{0:T(128)S(1)} %pad_add_fusion.refs_0_, s32[2,17,384]{2,1,0:T(8,128)S(1)} %copy-done, s32[2,17]{1,0:T(2,128)S(1)} %copy-done.1, f32[8,128,128]{2,1,0:T(8,128)S(1)} %collective-permute-done.6.refs_3_, f32[8,128,128]{2,1,0:T(8,128)S(1)} %collective-permute-done.3.refs_4_), custom_call_target="tpu_custom_call" | custom-call | flops 1000 | bytes 1000 | tf_op jit(solution)/shard_map/pallas_call | solution.py:193
  43.7 0.0 collective-permute-done.1
  43.7 6.7 %collective-permute-done.2 = f32[8,128,128]{2,1,0:T(8,128)S(1)} collective-permute-done((f32[8,128,128]{2,1,0:T(8,128)}, f32[8,128,128]{2,1,0:T(8,128)S(1)}, u32[]{:S(2)}, u32[]{:S(2)}) %collective-permute-start.2) | collective-permute-done | bytes 524320 | tf_op jit(solution)/shard_map/ppermute | solution.py:220
  50.4 0.1 broadcast_select_fusion.1.refs_3_
  50.5 0.0 collective-permute-done.4
  50.5 0.0 collective-permute-done.5
  50.5 0.1 broadcast_select_fusion.refs_4_
  50.6 4.0 %shard_map.30 = (f32[8,128,128]{2,1,0:T(8,128)S(1)}, f32[8,128,128]{2,1,0:T(8,128)S(1)}) custom-call(s32[3]{0:T(128)S(1)} %pad_add_fusion.refs_0_, s32[2,17,384]{2,1,0:T(8,128)S(1)} %copy-done, s32[2,17]{1,0:T(2,128)S(1)} %copy-done.1, f32[8,128,128]{2,1,0:T(8,128)S(1)} %broadcast_select_fusion.1.refs_3_, f32[8,128,128]{2,1,0:T(8,128)S(1)} %broadcast_select_fusion.refs_4_, ...), custom_call_target="tpu_custom_call" | custom-call | flops 1000 | bytes 1000 | tf_op jit(solution)/shard_map/pallas_call | solution.py:193
  54.6 1.9 %collective-permute-start.7 = (f32[8,128,128]{2,1,0:T(8,128)S(1)}, f32[8,128,128]{2,1,0:T(8,128)S(1)}, u32[]{:S(2)}, u32[]{:S(2)}) collective-permute-start(f32[8,128,128]{2,1,0:T(8,128)S(1)} %get-tuple-element.12), channel_id=1, source_target_pairs={{0,1},{1,0},{2,3},{3,2},{4,5},{5,4},{6,7},{7,6},{8,9},{9,8},{10,11... | collective-permute-start | bytes 1572872 | tf_op jit(solution)/shard_map/ppermute | solution.py:231
  56.5 1.9 %collective-permute-done.7 = f32[8,128,128]{2,1,0:T(8,128)S(1)} collective-permute-done((f32[8,128,128]{2,1,0:T(8,128)S(1)}, f32[8,128,128]{2,1,0:T(8,128)S(1)}, u32[]{:S(2)}, u32[]{:S(2)}) %collective-permute-start.7) | collective-permute-done | bytes 524320 | tf_op jit(solution)/shard_map/ppermute | solution.py:231
  58.4 0.9 %add_bitcast_fusion = f32[1,1,8,128,128]{4,3,2,1,0:T(8,128)} fusion(f32[8,128,128]{2,1,0:T(8,128)S(1)} %get-tuple-element.11, f32[8,128,128]{2,1,0:T(8,128)S(1)} %collective-permute-done.7), kind=kLoop, calls=%fused_computation | loop fusion | flops 131072 | bytes 1572864 | tf_op jit(solution)/shard_map/broadcast_in_dim | solution.py:231
Async XLA Ops:
  0.0 21.8 %collective-permute-start.3 = (f32[8,128,128]{2,1,0:T(8,128)}, f32[8,128,128]{2,1,0:T(8,128)S(1)}, u32[]{:S(2)}, u32[]{:S(2)}) collective-permute-start(f32[8,128,128]{2,1,0:T(8,128)} %bitcast.11), channel_id=1, source_target_pairs={{33,1},{67,3},{101,5},{135,7},{169,9},{203,11},{237,13},{271,15},{... | collective-permute-start | bytes 1572872 | tf_op jit(solution)/shard_map/ppermute | solution.py:217
  5.0 33.4 %collective-permute-start.6 = (f32[8,128,128]{2,1,0:T(8,128)}, f32[8,128,128]{2,1,0:T(8,128)S(1)}, u32[]{:S(2)}, u32[]{:S(2)}) collective-permute-start(f32[8,128,128]{2,1,0:T(8,128)} %bitcast.12), channel_id=1, source_target_pairs={{2,1},{4,3},{6,5},{8,7},{10,9},{12,11},{14,13},{16,15},{18,17},{20... | collective-permute-start | bytes 1572872 | tf_op jit(solution)/shard_map/ppermute | solution.py:218
  6.9 36.8 %collective-permute-start.1 = (f32[8,128,128]{2,1,0:T(8,128)}, f32[8,128,128]{2,1,0:T(8,128)S(1)}, u32[]{:S(2)}, u32[]{:S(2)}) collective-permute-start(f32[8,128,128]{2,1,0:T(8,128)} %bitcast.13), channel_id=1, source_target_pairs={{0,0},{2,2},{4,4},{6,6},{8,8},{10,10},{12,12},{14,14},{16,16},{18,... | collective-permute-start | bytes 1572872 | tf_op jit(solution)/shard_map/ppermute | solution.py:219
  12.2 38.2 %collective-permute-start.2 = (f32[8,128,128]{2,1,0:T(8,128)}, f32[8,128,128]{2,1,0:T(8,128)S(1)}, u32[]{:S(2)}, u32[]{:S(2)}) collective-permute-start(f32[8,128,128]{2,1,0:T(8,128)} %bitcast.14), channel_id=1, source_target_pairs={{4,1},{6,3},{8,5},{10,7},{12,9},{14,11},{16,13},{18,15},{20,17},{2... | collective-permute-start | bytes 1572872 | tf_op jit(solution)/shard_map/ppermute | solution.py:220
  19.9 13.0 %copy-start.2 = (s32[1,1,3,3,128]{4,3,1,2,0:T(4,128)}, s32[1,1,3,3,128]{4,3,1,2,0:T(4,128)S(1)}, u32[]{:S(2)}) copy-start(s32[1,1,3,3,128]{4,3,1,2,0:T(4,128)S(1)} %copy.5) | copy-start | bytes 13828
  19.9 11.0 %collective-permute-start = (s32[3,3,128]{2,1,0:T(4,128)S(1)}, s32[3,3,128]{2,1,0:T(4,128)S(1)}, u32[]{:S(2)}, u32[]{:S(2)}) collective-permute-start(s32[3,3,128]{2,1,0:T(4,128)S(1)} %bitcast.9), channel_id=1, source_target_pairs={{0,1},{1,0},{2,3},{3,2},{4,5},{5,4},{6,7},{7,6},{8,9},{9,8},{10,11... | collective-permute-start | bytes 13832 | tf_op jit(solution)/shard_map/ppermute | solution.py:224
  21.8 28.7 %collective-permute-start.4 = (f32[8,128,128]{2,1,0:T(8,128)S(1)}, f32[8,128,128]{2,1,0:T(8,128)S(1)}, u32[]{:S(2)}, u32[]{:S(2)}) collective-permute-start(f32[8,128,128]{2,1,0:T(8,128)S(1)} %collective-permute-done.3.refs_4_), channel_id=1, source_target_pairs={{481,0},{483,2},{485,4},{487,6},{489,8},{491,10},{493,12},{495,14}... | collective-permute-start | bytes 1572872 | tf_op jit(solution)/shard_map/ppermute | solution.py:221
  30.9 2.0 %copy-start.3 = (s32[3,3,128]{2,1,0:T(4,128)}, s32[3,3,128]{2,1,0:T(4,128)S(1)}, u32[]{:S(2)}) copy-start(s32[3,3,128]{2,1,0:T(4,128)S(1)} %collective-permute-done.other_ref) | copy-start | bytes 13828
  30.9 19.6 %collective-permute-start.5 = (f32[8,128,128]{2,1,0:T(8,128)S(1)}, f32[8,128,128]{2,1,0:T(8,128)S(1)}, u32[]{:S(2)}, u32[]{:S(2)}) collective-permute-start(f32[8,128,128]{2,1,0:T(8,128)S(1)} %collective-permute-done.3.refs_4_), channel_id=1, source_target_pairs={{33,1},{35,3},{37,5},{39,7},{41,9},{43,11},{45,13},{47,15},{49,17}... | collective-permute-start | bytes 1572872 | tf_op jit(solution)/shard_map/ppermute | solution.py:222
  38.4 0.7 %copy-start.1 = (s32[2,17]{1,0:T(2,128)S(1)}, s32[2,17]{1,0:T(2,128)}, u32[]{:S(2)}) copy-start(s32[2,17]{1,0:T(2,128)} %get-tuple-element.10.refs_2_) | copy-start | bytes 412
  39.0 0.9 %copy-start = (s32[2,17,384]{2,1,0:T(8,128)S(1)}, s32[2,17,384]{2,1,0:T(8,128)}, u32[]{:S(2)}) copy-start(s32[2,17,384]{2,1,0:T(8,128)} %get-tuple-element.9.refs_1_) | copy-start | bytes 156676
  54.6 3.8 %collective-permute-start.7 = (f32[8,128,128]{2,1,0:T(8,128)S(1)}, f32[8,128,128]{2,1,0:T(8,128)S(1)}, u32[]{:S(2)}, u32[]{:S(2)}) collective-permute-start(f32[8,128,128]{2,1,0:T(8,128)S(1)} %get-tuple-element.12), channel_id=1, source_target_pairs={{0,1},{1,0},{2,3},{3,2},{4,5},{5,4},{6,7},{7,6},{8,9},{9,8},{10,11... | collective-permute-start | bytes 1572872 | tf_op jit(solution)/shard_map/ppermute | solution.py:231

commit v3 on v2

v3 whole, which is shorter than its diff:
```python
import jax
import jax.numpy as jnp
from jax import lax
from jax.experimental import pallas as pl
from jax.experimental.pallas import tpu as pltpu
from jax.sharding import PartitionSpec as P

STEPS = 3
GRID = 16
SU = 8
BS = 128
NPAIR = 128
AXES = ("row", "col")


def device(r, j, core):
    return (r * GRID + j) * 2 + core


def data_core(a, b):
    return 0 if a <= b else 1


def left_route(step, to_core):
    return [
        (device(r, (r + j + step) % GRID, data_core(r, (r + j + step) % GRID)), device(r, j, to_core))
        for r in range(GRID)
        for j in range(GRID)
    ]


def right_route(step, to_core):
    return [
        (device((r + j + step) % GRID, j, data_core((r + j + step) % GRID, j)), device(r, j, to_core))
        for r in range(GRID)
        for j in range(GRID)
    ]


def near_route(shift, to_core):
    return [(device((r + shift) % GRID, j, 1), device(r, j, to_core)) for r in range(GRID) for j in range(GRID)]


def swap_route():
    return [(d, d ^ 1) for d in range(2 * GRID * GRID)]


def product_kernel(group, where_ref, lists_ref, *refs):
    if group == 0:
        left_in, right_in, acc_ref = refs[:3]
        sources = (None, (left_in, right_in))
    else:
        left0, left2, right0, right2, acc_ref, kept_ref, sent_ref = refs[:7]
        sources = ((left0, right0), (left2, right2))
    left_ref, right_ref, sems, lhs, rhs, prod, even_ref, odd_ref = refs[-8:]
    r = where_ref[0]
    j = where_ref[1]
    core = where_ref[2]
    step = 1 if group == 0 else 2 * core
    k = lax.rem(r + j + step, GRID)

    def halves(tile):
        high = tile.astype(jnp.bfloat16)
        return high, (tile - high.astype(jnp.float32)).astype(jnp.bfloat16)

    def load_left(flip):
        for x in range(SU):
            high, low = halves(left_ref[x].T if flip else left_ref[x])
            rows = slice(x * BS, (x + 1) * BS)
            lhs[rows, 0:BS] = high
            lhs[rows, BS : 2 * BS] = high
            lhs[rows, 2 * BS : 3 * BS] = low

    def load_right(flip):
        for y in range(SU):
            high, low = halves(right_ref[y].T if flip else right_ref[y])
            cols = slice(y * BS, (y + 1) * BS)
            rhs[0:BS, cols] = high
            rhs[BS : 2 * BS, cols] = low
            rhs[2 * BS : 3 * BS, cols] = high

    def multiply(v, w):
        for yp in range(SU // 2):
            b = rhs[:, yp * 2 * BS : (yp + 1) * 2 * BS]
            for xp in range(SU // 2):
                a = lhs[xp * 2 * BS : (xp + 1) * 2 * BS, :]
                res = jnp.dot(a, b, preferred_element_type=jnp.float32)
                rows = pl.ds(pl.multiple_of((v * SU + 2 * xp) * BS, BS), 2 * BS)
                prod[w * SU + 2 * yp, rows, :] = res[:, :BS]
                prod[w * SU + 2 * yp + 1, rows, :] = res[:, BS:]

    def copies(side):
        pair = sources[side]
        return [pltpu.make_async_copy(pair[n], (left_ref, right_ref)[n], sems.at[n]) for n in range(2)]

    def make_products():
        @pl.when(r <= k)
        def _():
            load_left(False)

        @pl.when(r > k)
        def _():
            load_left(True)

        copies(1)[1].wait()

        @pl.when(k <= j)
        def _():
            load_right(False)

        @pl.when(k > j)
        def _():
            load_right(True)

        v = (r > k).astype(jnp.int32)
        w = (k > j).astype(jnp.int32)
        multiply(v, w)

        @pl.when(r == k)
        def _():
            load_left(True)
            multiply(1, w)

        @pl.when(k == j)
        def _():
            load_right(True)
            multiply(jnp.where(r == k, 1, v), 1)

            @pl.when(r == k)
            def _():
                load_left(False)
                multiply(0, 1)

    def add_products(side):
        ref = lists_ref.at[side]
        count = jnp.int32(0)
        jump = NPAIR
        while jump:
            at = jnp.minimum(count + jump, NPAIR) - 1
            real = jnp.logical_and(count + jump <= NPAIR, ref[step, 2, at] < 2 * SU)
            count = jnp.where(real, count + jump, count)
            jump //= 2

        def add(i, acc):
            x = jnp.minimum(ref[step, 0, i], 2 * SU - 1)
            y = jnp.minimum(ref[step, 1, i], 2 * SU - 1)
            t = jnp.bitwise_xor(ref[step, 2, i], core * SU)
            acc[t] = acc[t] + prod[y, pl.ds(pl.multiple_of(x * BS, BS), BS), :]

        def four(i, carry):
            for n in range(4):
                add(4 * i + n, (even_ref, odd_ref)[n % 2])
            return carry

        def one(i, carry):
            add(i, even_ref)
            return carry

        lax.fori_loop(0, count // 4, four, 0)
        lax.fori_loop(count - count % 4, count, one, 0)

    def run():
        even_ref[...] = jnp.zeros_like(even_ref)
        odd_ref[...] = jnp.zeros_like(odd_ref)
        copies(1)[0].wait()
        make_products()
        add_products(0)
        add_products(1)

    for side in range(2):
        if sources[side] is not None:

            @pl.when(core == side)
            def _(side=side):
                for copy in copies(side):
                    copy.start()

    if group == 0:

        @pl.when(core == 0)
        def _():
            acc_ref[...] = jnp.zeros_like(acc_ref)

        @pl.when(core == 1)
        def _():
            run()
            for t in range(2 * SU):
                acc_ref[t] = even_ref[t] + odd_ref[t]

    else:
        run()
        for t in range(SU):
            sent_ref[t] = even_ref[SU + t] + odd_ref[SU + t] + acc_ref[SU + t]
        for t in range(SU):
            kept_ref[t] = even_ref[t] + odd_ref[t] + acc_ref[t]


def product(group, where, lists, panels, acc):
    smem = pl.BlockSpec(memory_space=pltpu.SMEM)
    vmem = pl.BlockSpec(memory_space=pltpu.VMEM)
    hbm = pl.BlockSpec(memory_space=pl.ANY)
    out = jax.ShapeDtypeStruct(((2 - group) * SU, BS, BS), jnp.float32)

    def kernel(*refs):
        product_kernel(group, *refs)

    return pl.pallas_call(
        kernel,
        out_shape=(out,) * (1 + group),
        in_specs=[smem] * 2 + [hbm] * len(panels) + [vmem] * len(acc),
        out_specs=(vmem,) * (1 + group),
        scratch_shapes=[
            pltpu.VMEM((SU, BS, BS), jnp.float32),
            pltpu.VMEM((SU, BS, BS), jnp.float32),
            pltpu.SemaphoreType.DMA((2,)),
            pltpu.VMEM((SU * BS, 3 * BS), jnp.bfloat16),
            pltpu.VMEM((3 * BS, SU * BS), jnp.bfloat16),
            pltpu.VMEM((2 * SU, 2 * SU * BS, BS), jnp.float32),
            pltpu.VMEM((2 * SU, BS, BS), jnp.float32),
            pltpu.VMEM((2 * SU, BS, BS), jnp.float32),
        ],
        compiler_params=pltpu.CompilerParams(vmem_limit_bytes=36 * 1024 * 1024),
        cost_estimate=pl.CostEstimate(flops=1000, bytes_accessed=1000, transcendentals=0),
    )(where, lists, *panels, *acc)


def on_device(stored, pair_lists):
    r = lax.axis_index("row")
    c = lax.axis_index("col")
    j = c // 2
    core = c % 2
    mine = stored[0, 0]
    lists = pair_lists[0, 0]

    middle = lax.ppermute(mine, AXES, right_route(1, 1))
    left1 = lax.ppermute(mine, AXES, left_route(1, 1))
    left0 = lax.ppermute(mine, AXES, left_route(0, 0))
    left2 = lax.ppermute(mine, AXES, left_route(2, 1))
    right0 = lax.ppermute(middle, AXES, near_route(-1, 0))
    right2 = lax.ppermute(middle, AXES, near_route(1, 1))

    both = jnp.stack([lists, lax.ppermute(lists, AXES, swap_route())])
    where = jnp.stack([r, j, core]).astype(jnp.int32)
    acc = product(0, where, both, (left1, middle), ())
    kept, sent = product(1, where, both, (left0, left2, right0, right2), acc)
    return (kept + lax.ppermute(sent, AXES, swap_route()))[None, None]


def solution(mesh):
    return jax.shard_map(
        on_device,
        mesh=mesh,
        in_specs=(P("row", "col", None, None, None), P("row", "col", None, None, None)),
        out_specs=P("row", "col", None, None, None),
        check_vma=False,
    )
```

time: 59.7 us -> 59.6 us (level)
  waiting for transfers between devices: 8.63 us -> 18.9 us
  Pallas kernels: 13.1 us -> 7.86 us
  starting transfers between devices: 34 us -> 30.1 us
  local copies, waits for them, and re-layouts: 2.24 us -> 1.38 us
    ppermute x1, waiting for transfers between devices: 6.74 us -> 15.1 us  [on_device(): left2 = lax.ppermute(mine, AXES, left_route(2, 1))]
    ppermute x1, starting transfers between devices: 9.07 us -> 1.32 us  [on_device(): right0 = lax.ppermute(middle, AXES, near_route(-1, 0))]
    ppermute x1, starting transfers between devices: 1.92 us -> 7.42 us  [on_device(): right2 = lax.ppermute(middle, AXES, near_route(1, 1))]
    pallas_call x3 -> x2, Pallas kernels: 13.1 us -> 7.86 us  [product(): pl.pallas_call(kernel, out_shape=(out,) * (1 + group), in_specs=[smem] *...]
    ppermute x1, starting transfers between devices: 5.3 us -> 1.32 us  [on_device(): left0 = lax.ppermute(mine, AXES, left_route(0, 0))]
    ppermute x1, waiting for transfers between devices: 0.01 us -> 1.94 us  [on_device(): left1 = lax.ppermute(mine, AXES, left_route(1, 1))]
    ppermute x1, starting transfers between devices: 1.92 us -> 3.37 us  [on_device(): left1 = lax.ppermute(mine, AXES, left_route(1, 1))]
    ppermute x1, starting transfers between devices: 6.97 us -> 7.88 us  [on_device(): left2 = lax.ppermute(mine, AXES, left_route(2, 1))]
  transfers between devices with their start and end apart: 8 -> 8, of which waited for: 2 -> 3; matrix products, arithmetic and copies ran while one was open for 1% -> 1% of each run, Pallas kernels for 15% -> 6%
where the time goes in v3:
time: 59.6 us; the launch traced here: 59.4 us
  starting transfers between devices  30.1 us (51%)
  waiting for transfers between devices  18.9 us (32%)
  Pallas kernels  7.86 us (13%)
  local copies, waits for them, and re-layouts  1.38 us (2%)
  other arithmetic  0.95 us (2%)
    ppermute x1, waiting for transfers between devices, on_device(): left2 = lax.ppermute(mine, AXES, left_route(2, 1))  15.1 us
    ppermute x1, starting transfers between devices, on_device(): left2 = lax.ppermute(mine, AXES, left_route(2, 1))  7.88 us
    pallas_call x2, Pallas kernels, product(): pl.pallas_call(kernel, out_shape=(out,) * (1 + group), in_specs=[smem] *...  7.86 us
    ppermute x1, starting transfers between devices, on_device(): right2 = lax.ppermute(middle, AXES, near_route(1, 1))  7.42 us
    ppermute x1, starting transfers between devices, on_device(): middle = lax.ppermute(mine, AXES, right_route(1, 1))  4.96 us
    ppermute x1, starting transfers between devices, on_device(): left1 = lax.ppermute(mine, AXES, left_route(1, 1))  3.37 us
    ppermute x1, waiting for transfers between devices, on_device(): left1 = lax.ppermute(mine, AXES, left_route(1, 1))  1.94 us
    ppermute x1, starting transfers between devices, on_device(): return (kept + lax.ppermute(sent, AXES, swap_route()))[None, None]  1.92 us
  transfers between devices with their start and end apart: 8, of which 3 were waited for; matrix products, arithmetic and copies ran while one was open for 1% of the time, Pallas kernels for 6%

profile of v3, /device:TPU:193, one launch (start us, length us, event | category | flops | bytes accessed | tf_op | source)
XLA Modules:
  0.0 59.4 jit_solution(10110356825484926398)
XLA Ops:
  0.0 5.0 %collective-permute-start.3 = (f32[8,128,128]{2,1,0:T(8,128)}, f32[8,128,128]{2,1,0:T(8,128)S(1)}, u32[]{:S(2)}, u32[]{:S(2)}) collective-permute-start(f32[8,128,128]{2,1,0:T(8,128)} %bitcast.14), channel_id=1, source_target_pairs={{33,1},{67,3},{101,5},{135,7},{169,9},{203,11},{237,13},{271,15},{... | collective-permute-start | bytes 1572872 | tf_op jit(solution)/shard_map/ppermute | solution.py:235
  5.0 0.7 %copy.6 = s32[1,1,3,3,128]{4,3,1,2,0:T(4,128)S(1)} copy(s32[1,1,3,3,128]{4,1,3,2,0:T(1,128)} %param.3) | data formatting | bytes 9216
  5.7 1.9 %collective-permute-start = (s32[3,3,128]{2,1,0:T(4,128)S(1)}, s32[3,3,128]{2,1,0:T(4,128)S(1)}, u32[]{:S(2)}, u32[]{:S(2)}) collective-permute-start(s32[3,3,128]{2,1,0:T(4,128)S(1)} %bitcast.13), channel_id=1, source_target_pairs={{0,1},{1,0},{2,3},{3,2},{4,5},{5,4},{6,7},{7,6},{8,9},{9,8},{10,11... | collective-permute-start | bytes 13832 | tf_op jit(solution)/shard_map/ppermute | solution.py:242
  7.6 3.4 %collective-permute-start.6 = (f32[8,128,128]{2,1,0:T(8,128)}, f32[8,128,128]{2,1,0:T(8,128)S(1)}, u32[]{:S(2)}, u32[]{:S(2)}) collective-permute-start(f32[8,128,128]{2,1,0:T(8,128)} %bitcast.15), channel_id=1, source_target_pairs={{2,1},{4,3},{6,5},{8,7},{10,9},{12,11},{14,13},{16,15},{18,17},{20... | collective-permute-start | bytes 1572872 | tf_op jit(solution)/shard_map/ppermute | solution.py:236
  11.0 7.9 %collective-permute-start.2 = (f32[8,128,128]{2,1,0:T(8,128)}, f32[8,128,128]{2,1,0:T(8,128)S(1)}, u32[]{:S(2)}, u32[]{:S(2)}) collective-permute-start(f32[8,128,128]{2,1,0:T(8,128)} %bitcast.16), channel_id=1, source_target_pairs={{4,1},{6,3},{8,5},{10,7},{12,9},{14,11},{16,13},{18,15},{20,17},{2... | collective-permute-start | bytes 1572872 | tf_op jit(solution)/shard_map/ppermute | solution.py:238
  18.8 1.3 %collective-permute-start.1 = (f32[8,128,128]{2,1,0:T(8,128)}, f32[8,128,128]{2,1,0:T(8,128)S(1)}, u32[]{:S(2)}, u32[]{:S(2)}) collective-permute-start(f32[8,128,128]{2,1,0:T(8,128)} %bitcast.17), channel_id=1, source_target_pairs={{0,0},{2,2},{4,4},{6,6},{8,8},{10,10},{12,12},{14,14},{16,16},{18,... | collective-permute-start | bytes 1572872 | tf_op jit(solution)/shard_map/ppermute | solution.py:237
  20.2 0.0 collective-permute-done.3.refs_3_
  20.2 7.4 %collective-permute-start.5 = (f32[8,128,128]{2,1,0:T(8,128)S(1)}, f32[8,128,128]{2,1,0:T(8,128)S(1)}, u32[]{:S(2)}, u32[]{:S(2)}) collective-permute-start(f32[8,128,128]{2,1,0:T(8,128)S(1)} %collective-permute-done.3.refs_3_), channel_id=1, source_target_pairs={{33,1},{35,3},{37,5},{39,7},{41,9},{43,11},{45,13},{47,15},{49,17}... | collective-permute-start | bytes 1572872 | tf_op jit(solution)/shard_map/ppermute | solution.py:240
  27.6 0.0 collective-permute-done
  27.6 1.3 %collective-permute-start.4 = (f32[8,128,128]{2,1,0:T(8,128)S(1)}, f32[8,128,128]{2,1,0:T(8,128)S(1)}, u32[]{:S(2)}, u32[]{:S(2)}) collective-permute-start(f32[8,128,128]{2,1,0:T(8,128)S(1)} %collective-permute-done.3.refs_3_), channel_id=1, source_target_pairs={{481,0},{483,2},{485,4},{487,6},{489,8},{491,10},{493,12},{495,14}... | collective-permute-start | bytes 1572872 | tf_op jit(solution)/shard_map/ppermute | solution.py:239
  29.0 0.0 copy-start
  29.0 0.7 %copy-done = s32[1,1,3,3,128]{4,1,3,2,0:T(1,128)S(1)} copy-done((s32[1,1,3,3,128]{4,1,3,2,0:T(1,128)S(1)}, s32[1,1,3,3,128]{4,1,3,2,0:T(1,128)}, u32[]{:S(2)}) %copy-start) | copy-done | bytes 4632
  29.7 0.1 pad_add_fusion.1.refs_0_
  29.7 1.9 %collective-permute-done.6.refs_2_ = f32[8,128,128]{2,1,0:T(8,128)S(1)} collective-permute-done((f32[8,128,128]{2,1,0:T(8,128)}, f32[8,128,128]{2,1,0:T(8,128)S(1)}, u32[]{:S(2)}, u32[]{:S(2)}) %collective-permute-start.6) | collective-permute-done | bytes 524320 | tf_op jit(solution)/shard_map/ppermute | solution.py:236
  31.7 3.9 %shard_map.28.refs_6_ = f32[16,128,128]{2,1,0:T(8,128)S(1)} custom-call(s32[3]{0:T(128)S(1)} %pad_add_fusion.1.refs_0_, s32[2,3,3,128]{3,2,1,0:T(4,128)S(1)} %pad_add_fusion.refs_1_, f32[8,128,128]{2,1,0:T(8,128)S(1)} %collective-permute-done.6.refs_2_, f32[8,128,128]{2,1,0:T(8,128)S(1)} %collective-permute-done.3.refs_3_), custom_call_target="tpu_custom_call" | custom-call | flops 1000 | bytes 1000 | tf_op jit(solution)/shard_map/pallas_call | solution.py:207
  35.5 15.1 %collective-permute-done.2.refs_3_ = f32[8,128,128]{2,1,0:T(8,128)S(1)} collective-permute-done((f32[8,128,128]{2,1,0:T(8,128)}, f32[8,128,128]{2,1,0:T(8,128)S(1)}, u32[]{:S(2)}, u32[]{:S(2)}) %collective-permute-start.2) | collective-permute-done | bytes 524320 | tf_op jit(solution)/shard_map/ppermute | solution.py:238
  50.7 0.0 collective-permute-done.1.refs_2_
  50.7 0.0 collective-permute-done.5.refs_5_
  50.7 0.0 collective-permute-done.4.refs_4_
  50.7 4.0 %shard_map.29 = (f32[8,128,128]{2,1,0:T(8,128)S(1)}, f32[8,128,128]{2,1,0:T(8,128)S(1)}) custom-call(s32[3]{0:T(128)S(1)} %pad_add_fusion.1.refs_0_, s32[2,3,3,128]{3,2,1,0:T(4,128)S(1)} %pad_add_fusion.refs_1_, f32[8,128,128]{2,1,0:T(8,128)S(1)} %collective-permute-done.1.refs_2_, f32[8,128,128]{2,1,0:T(8,128)S(1)} %collective-permute-done.2.refs_3_, ...), custom_call_target="tpu_custom_call" | custom-call | flops 1000 | bytes 1000 | tf_op jit(solution)/shard_map/pallas_call | solution.py:207
  54.7 1.9 %collective-permute-start.7 = (f32[8,128,128]{2,1,0:T(8,128)S(1)}, f32[8,128,128]{2,1,0:T(8,128)S(1)}, u32[]{:S(2)}, u32[]{:S(2)}) collective-permute-start(f32[8,128,128]{2,1,0:T(8,128)S(1)} %get-tuple-element.8), channel_id=1, source_target_pairs={{0,1},{1,0},{2,3},{3,2},{4,5},{5,4},{6,7},{7,6},{8,9},{9,8},{10,11... | collective-permute-start | bytes 1572872 | tf_op jit(solution)/shard_map/ppermute | solution.py:246
  56.6 1.9 %collective-permute-done.7 = f32[8,128,128]{2,1,0:T(8,128)S(1)} collective-permute-done((f32[8,128,128]{2,1,0:T(8,128)S(1)}, f32[8,128,128]{2,1,0:T(8,128)S(1)}, u32[]{:S(2)}, u32[]{:S(2)}) %collective-permute-start.7) | collective-permute-done | bytes 524320 | tf_op jit(solution)/shard_map/ppermute | solution.py:246
  58.5 0.9 %add_bitcast_fusion = f32[1,1,8,128,128]{4,3,2,1,0:T(8,128)} fusion(f32[8,128,128]{2,1,0:T(8,128)S(1)} %get-tuple-element.7, f32[8,128,128]{2,1,0:T(8,128)S(1)} %collective-permute-done.7), kind=kLoop, calls=%fused_computation | loop fusion | flops 131072 | bytes 1572864 | tf_op jit(solution)/shard_map/broadcast_in_dim | solution.py:246
  (2 shorter events, 0.0 us)
Async XLA Ops:
  0.0 20.2 %collective-permute-start.3 = (f32[8,128,128]{2,1,0:T(8,128)}, f32[8,128,128]{2,1,0:T(8,128)S(1)}, u32[]{:S(2)}, u32[]{:S(2)}) collective-permute-start(f32[8,128,128]{2,1,0:T(8,128)} %bitcast.14), channel_id=1, source_target_pairs={{33,1},{67,3},{101,5},{135,7},{169,9},{203,11},{237,13},{271,15},{... | collective-permute-start | bytes 1572872 | tf_op jit(solution)/shard_map/ppermute | solution.py:235
  5.7 21.9 %collective-permute-start = (s32[3,3,128]{2,1,0:T(4,128)S(1)}, s32[3,3,128]{2,1,0:T(4,128)S(1)}, u32[]{:S(2)}, u32[]{:S(2)}) collective-permute-start(s32[3,3,128]{2,1,0:T(4,128)S(1)} %bitcast.13), channel_id=1, source_target_pairs={{0,1},{1,0},{2,3},{3,2},{4,5},{5,4},{6,7},{7,6},{8,9},{9,8},{10,11... | collective-permute-start | bytes 13832 | tf_op jit(solution)/shard_map/ppermute | solution.py:242
  7.6 24.1 %collective-permute-start.6 = (f32[8,128,128]{2,1,0:T(8,128)}, f32[8,128,128]{2,1,0:T(8,128)S(1)}, u32[]{:S(2)}, u32[]{:S(2)}) collective-permute-start(f32[8,128,128]{2,1,0:T(8,128)} %bitcast.15), channel_id=1, source_target_pairs={{2,1},{4,3},{6,5},{8,7},{10,9},{12,11},{14,13},{16,15},{18,17},{20... | collective-permute-start | bytes 1572872 | tf_op jit(solution)/shard_map/ppermute | solution.py:236
  11.0 39.7 %collective-permute-start.2 = (f32[8,128,128]{2,1,0:T(8,128)}, f32[8,128,128]{2,1,0:T(8,128)S(1)}, u32[]{:S(2)}, u32[]{:S(2)}) collective-permute-start(f32[8,128,128]{2,1,0:T(8,128)} %bitcast.16), channel_id=1, source_target_pairs={{4,1},{6,3},{8,5},{10,7},{12,9},{14,11},{16,13},{18,15},{20,17},{2... | collective-permute-start | bytes 1572872 | tf_op jit(solution)/shard_map/ppermute | solution.py:238
  18.8 31.8 %collective-permute-start.1 = (f32[8,128,128]{2,1,0:T(8,128)}, f32[8,128,128]{2,1,0:T(8,128)S(1)}, u32[]{:S(2)}, u32[]{:S(2)}) collective-permute-start(f32[8,128,128]{2,1,0:T(8,128)} %bitcast.17), channel_id=1, source_target_pairs={{0,0},{2,2},{4,4},{6,6},{8,8},{10,10},{12,12},{14,14},{16,16},{18,... | collective-permute-start | bytes 1572872 | tf_op jit(solution)/shard_map/ppermute | solution.py:237
  20.2 30.5 %collective-permute-start.5 = (f32[8,128,128]{2,1,0:T(8,128)S(1)}, f32[8,128,128]{2,1,0:T(8,128)S(1)}, u32[]{:S(2)}, u32[]{:S(2)}) collective-permute-start(f32[8,128,128]{2,1,0:T(8,128)S(1)} %collective-permute-done.3.refs_3_), channel_id=1, source_target_pairs={{33,1},{35,3},{37,5},{39,7},{41,9},{43,11},{45,13},{47,15},{49,17}... | collective-permute-start | bytes 1572872 | tf_op jit(solution)/shard_map/ppermute | solution.py:240
  27.6 23.0 %collective-permute-start.4 = (f32[8,128,128]{2,1,0:T(8,128)S(1)}, f32[8,128,128]{2,1,0:T(8,128)S(1)}, u32[]{:S(2)}, u32[]{:S(2)}) collective-permute-start(f32[8,128,128]{2,1,0:T(8,128)S(1)} %collective-permute-done.3.refs_3_), channel_id=1, source_target_pairs={{481,0},{483,2},{485,4},{487,6},{489,8},{491,10},{493,12},{495,14}... | collective-permute-start | bytes 1572872 | tf_op jit(solution)/shard_map/ppermute | solution.py:239
  29.0 0.7 %copy-start = (s32[1,1,3,3,128]{4,1,3,2,0:T(1,128)S(1)}, s32[1,1,3,3,128]{4,1,3,2,0:T(1,128)}, u32[]{:S(2)}) copy-start(s32[1,1,3,3,128]{4,1,3,2,0:T(1,128)} %param.3) | copy-start | bytes 13828
  54.7 3.8 %collective-permute-start.7 = (f32[8,128,128]{2,1,0:T(8,128)S(1)}, f32[8,128,128]{2,1,0:T(8,128)S(1)}, u32[]{:S(2)}, u32[]{:S(2)}) collective-permute-start(f32[8,128,128]{2,1,0:T(8,128)S(1)} %get-tuple-element.8), channel_id=1, source_target_pairs={{0,1},{1,0},{2,3},{3,2},{4,5},{5,4},{6,7},{7,6},{8,9},{9,8},{10,11... | collective-permute-start | bytes 1572872 | tf_op jit(solution)/shard_map/ppermute | solution.py:246
